TPU v7x, 32 devices: a whole 2x2x4 slice. The times are simulated.
32 devices in a mesh: section: 4 (over y, x), dp: 8 (over z, core).
Axes of the slice: x: 2, y: 2, z: 4, core: 2. Of those that a mesh axis runs over, the one named last changes fastest.
Arguments:
- inputs: bfloat16 [48, 512, 768], P('dp'), may hold values from -6 to 6
- bucket: int32 [48], P('dp'), may hold values from 0 to 3, as said below
- padding: int32 [48, 512], P('dp'), may hold values from 0 to 1, as said below
- cotangent: bfloat16 [48, 512, 768], P('dp'), may hold values from -6 to 6
- down_weight: bfloat16 [4, 768, 64], P('section'), may hold values from -0.21875 to 0.21875
- down_bias: float32 [4, 64], P('section'), may hold values from -3 to 3
- up_weight: bfloat16 [4, 64, 768], P('section'), may hold values from -0.75 to 0.75
- up_bias: float32 [4, 768], P('section'), may hold values from -2 to 2
- ln_gain: float32 [4, 768], P('section'), may hold values from 0.1 to 1.9
- ln_beta: float32 [4, 768], P('section'), may hold values from -2 to 2
- qkv_weight: bfloat16 [2, 768, 2304], P(None, 'dp'), may hold values from -0.21875 to 0.21875
- query_bias: float32 [2, 768], replicated, may hold values from -2 to 2
- value_bias: float32 [2, 768], replicated, may hold values from -2 to 2
- attn_out_weight: bfloat16 [2, 768, 768], P(None, 'dp'), may hold values from -1.25 to 1.25
- attn_out_bias: float32 [2, 768], replicated, may hold values from -2 to 2
- ffn_in_weight: bfloat16 [2, 768, 3072], P(None, 'dp'), may hold values from -0.21875 to 0.21875
- ffn_in_bias: float32 [2, 3072], replicated, may hold values from -2 to 2
- ffn_out_weight: bfloat16 [2, 3072, 768], P(None, 'dp'), may hold values from -0.15625 to 0.15625
- ffn_out_bias: float32 [2, 768], replicated, may hold values from -2 to 2
Outputs:
- sub_outputs: bfloat16 [4, 48, 512, 768], P('section', 'dp')
- sub_input_grads: bfloat16 [4, 48, 512, 768], P('section', 'dp')
- grad_down_weight: float32 [4, 768, 64], P('section')
- grad_down_bias: float32 [4, 64], P('section')
- grad_up_weight: float32 [4, 64, 768], P('section')
- grad_up_bias: float32 [4, 768], P('section')
- grad_ln_gain: float32 [4, 768], P('section')
- grad_ln_beta: float32 [4, 768], P('section')
- ratios: float32 [4], P('section')
Inputs may be any that keep to these rules, and one draw needn't show every extreme that they name: A row holds sequences of 64 * 2**bucket positions each, one after the other. `padding`: within each sequence of a row the ones come first, and each sequence has at least one.
All inputs are finite; a program needn't handle non-finite values.
Results may differ from a plain program's by a relative error of at most 0.024.
Values may be sent and summed in bfloat16 or wider, within the bound.
A program may use at most 320 MiB of HBM per device.

v0:
```python
import jax
import jax.numpy as jnp
from jax import lax
from jax.sharding import PartitionSpec as P

HEADS = 12
HD = 64
SEG = 64


EPSILON = 1e-05
MASKED = -1e30


def from_behind(value, axis, steps):
    count = lax.axis_size(axis)
    initial, last = (max(0, -steps), min(count, count - steps))
    return lax.ppermute(value, axis, [(source, source + steps) for source in range(initial, last)])


def product(left, right):
    return jnp.dot(left, right, preferred_element_type=jnp.float32)


def times_transposed(left, right):
    return lax.dot_general(
        left, right, (((1,), (1,)), ((), ())), preferred_element_type=jnp.float32
    )


def transposed_times(left, right):
    return lax.dot_general(
        left, right, (((0,), (0,)), ((), ())), preferred_element_type=jnp.float32
    )


def gelu_value(values):
    return jax.nn.gelu(values, approximate=False)


def gelu_slope(values):
    return (
        0.5 * (1.0 + lax.erf(values * 0.7071067811865476))
        + values * jnp.exp(-0.5 * values * values) * 0.3989422804014327
    )


def norm_parts(resid):
    center = resid - jnp.mean(resid, -1, keepdims=True)
    inverse = lax.rsqrt(jnp.mean(center * center, -1, keepdims=True) + EPSILON)
    return (center * inverse, inverse)


def key_rules(bucket_id, pad_row, length):
    seq_span = SEG * jnp.left_shift(jnp.int32(1), bucket_id)
    places = jnp.arange(length, dtype=jnp.int32)
    same_piece = places[:, None] // seq_span == places[None, :] // seq_span
    return same_piece & (pad_row[None, :] == 1)


def split_heads(matrix):
    return matrix.reshape(matrix.shape[0], HEADS, HD)


def scores_of(qkv_low, allowed):
    width = qkv_low.shape[1] // 3
    query_heads = split_heads(qkv_low[:, :width])
    key_heads = split_heads(qkv_low[:, width : 2 * width])
    raw_scores = jnp.einsum(
        "qhd,khd->hqk", query_heads, key_heads, preferred_element_type=jnp.float32
    ) * HD ** (-0.5)
    return jnp.where(allowed[None], raw_scores, MASKED)


def attention_forward(hidden, allowed, qkv_full, query_shift, value_shift):
    width = hidden.shape[1]
    length = hidden.shape[0]
    mixed = product(hidden, qkv_full)
    query_low = (mixed[:, :width] + query_shift).astype(jnp.bfloat16)
    keys_low = mixed[:, width : 2 * width].astype(jnp.bfloat16)
    values_low = (mixed[:, 2 * width :] + value_shift).astype(jnp.bfloat16)
    qkv_low = jnp.concatenate([query_low, keys_low, values_low], 1)
    scores = scores_of(qkv_low, allowed)
    peak = jnp.max(scores, -1, keepdims=True)
    expo = jnp.exp(scores - peak)
    totals = jnp.sum(expo, -1, keepdims=True)
    log_total = (peak + jnp.log(totals))[:, :, 0]
    probs_low = (expo / totals).astype(jnp.bfloat16)
    attended = jnp.einsum(
        "hqk,khd->qhd", probs_low, split_heads(values_low), preferred_element_type=jnp.float32
    )
    return (qkv_low, log_total, attended.reshape(length, width).astype(jnp.bfloat16))


def on_device(
    inputs,
    bucket,
    padding,
    cotangent,
    down_weight,
    down_bias,
    up_weight,
    up_bias,
    ln_gain,
    ln_beta,
    qkv_weight,
    query_bias,
    value_bias,
    attn_out_weight,
    attn_out_bias,
    ffn_in_weight,
    ffn_in_bias,
    ffn_out_weight,
    ffn_out_bias,
):
    section_index = lax.axis_index("section")
    section_count = lax.axis_size("section")
    micro = inputs.shape[0]
    length = inputs.shape[1]
    width = inputs.shape[2]
    ffn_width = ffn_in_weight.shape[2]
    adapter_width = down_weight.shape[2]
    is_attention = section_index % 2 == 0
    layer_index = section_index // 2

    def pick(stacked):
        return lax.dynamic_index_in_dim(stacked, layer_index, 0, keepdims=False)

    query_shift = pick(query_bias)
    value_shift = pick(value_bias)
    attn_shift = pick(attn_out_bias)
    ffn_in_shift = pick(ffn_in_bias)
    ffn_out_shift = pick(ffn_out_bias)
    adapter = (down_weight[0], down_bias[0], up_weight[0], up_bias[0], ln_gain[0], ln_beta[0])

    def empty_keep():
        return (
            jnp.zeros((length, 3 * width), jnp.bfloat16),
            jnp.zeros((HEADS, length), jnp.float32),
            jnp.zeros((length, width), jnp.bfloat16),
            jnp.zeros((length, ffn_width), jnp.float32),
            jnp.zeros((length, width), jnp.float32),
            jnp.zeros((length, adapter_width), jnp.float32),
            jnp.zeros((length, width), jnp.float32),
        )

    def masks(slot_index):
        bucket_id = lax.dynamic_index_in_dim(bucket, slot_index, 0, keepdims=False)
        pad_row = lax.dynamic_index_in_dim(padding, slot_index, 0, keepdims=False)
        return (key_rules(bucket_id, pad_row, length), pad_row.astype(jnp.float32))

    def store(buffer, slot_index, fresh, is_valid):
        previous = lax.dynamic_index_in_dim(buffer, slot_index, 0, keepdims=False)
        return lax.dynamic_update_index_in_dim(
            buffer, jnp.where(is_valid, fresh, previous), slot_index, 0
        )

    def forward_step(frozen, hidden, allowed, valid_row):
        qkv_full, attn_full, ffn_in_full, ffn_out_full = frozen

        def forward_attention_case():
            qkv_low, log_total, attended = attention_forward(
                hidden, allowed, qkv_full, query_shift, value_shift
            )
            branch = product(attended, attn_full) + attn_shift
            return (
                branch,
                qkv_low,
                log_total,
                attended,
                jnp.zeros((length, ffn_width), jnp.float32),
            )

        def forward_ffn_case():
            pre_act = product(hidden, ffn_in_full) + ffn_in_shift
            branch = product(gelu_value(pre_act).astype(jnp.bfloat16), ffn_out_full) + ffn_out_shift
            return (
                branch,
                jnp.zeros((length, 3 * width), jnp.bfloat16),
                jnp.zeros((HEADS, length), jnp.float32),
                jnp.zeros((length, width), jnp.bfloat16),
                pre_act,
            )

        branch, qkv_low, log_total, attended, pre_act = lax.cond(
            is_attention, forward_attention_case, forward_ffn_case
        )
        down_matrix, down_shift, lift_matrix, lift_shift, norm_gain, norm_shift = adapter
        hidden_float = hidden.astype(jnp.float32)
        down_act = product(branch.astype(jnp.bfloat16), down_matrix) + down_shift
        lifted = product(gelu_value(down_act).astype(jnp.bfloat16), lift_matrix) + lift_shift
        resid = hidden_float + branch + lifted
        normed, inverse = norm_parts(resid)
        output = (normed * norm_gain + norm_shift).astype(jnp.bfloat16)
        square_sums = jnp.stack(
            [
                jnp.sum(valid_row * jnp.sum(lifted * lifted, -1)),
                jnp.sum(valid_row * jnp.sum(hidden_float * hidden_float, -1)),
            ]
        )
        return (
            output,
            (qkv_low, log_total, attended, pre_act, branch, down_act, resid),
            square_sums,
        )

    def backward_step(frozen, grad_out, keep, allowed):
        qkv_full, attn_full, ffn_in_full, ffn_out_full = frozen
        qkv_low, log_total, attended, pre_act, branch, down_act, resid = keep
        down_matrix, down_shift, lift_matrix, lift_shift, norm_gain, norm_shift = adapter
        upstream = grad_out.astype(jnp.float32)
        normed, inverse = norm_parts(resid)
        grad_gain = jnp.sum(normed * upstream, 0)
        grad_shift = jnp.sum(upstream, 0)
        scaled = upstream * norm_gain
        grad_resid = inverse * (
            scaled
            - jnp.mean(scaled, -1, keepdims=True)
            - normed * jnp.mean(scaled * normed, -1, keepdims=True)
        )
        lift_grad = grad_resid.astype(jnp.bfloat16)
        grad_lift_matrix = transposed_times(gelu_value(down_act).astype(jnp.bfloat16), lift_grad)
        grad_lift_shift = jnp.sum(lift_grad.astype(jnp.float32), 0)
        down_grad = (times_transposed(lift_grad, lift_matrix) * gelu_slope(down_act)).astype(
            jnp.bfloat16
        )
        grad_down_matrix = transposed_times(branch.astype(jnp.bfloat16), down_grad)
        grad_down_shift = jnp.sum(down_grad.astype(jnp.float32), 0)
        branch_grad = (grad_resid + times_transposed(down_grad, down_matrix)).astype(jnp.bfloat16)

        def backward_attention_case():
            attended_grad = split_heads(
                times_transposed(branch_grad, attn_full).astype(jnp.bfloat16)
            )
            scores = scores_of(qkv_low, allowed)
            probs = jnp.exp(scores - log_total[:, :, None])
            probs_low = probs.astype(jnp.bfloat16)
            query_heads = split_heads(qkv_low[:, :width])
            key_heads = split_heads(qkv_low[:, width : 2 * width])
            value_heads = split_heads(qkv_low[:, 2 * width :])
            grad_values = jnp.einsum(
                "hqk,qhd->khd", probs_low, attended_grad, preferred_element_type=jnp.float32
            )
            grad_probs = jnp.einsum(
                "qhd,khd->hqk", attended_grad, value_heads, preferred_element_type=jnp.float32
            )
            row_dot = jnp.sum(probs * grad_probs, -1, keepdims=True)
            score_grad = (probs * (grad_probs - row_dot)).astype(jnp.bfloat16)
            grad_query = jnp.einsum(
                "hqk,khd->qhd", score_grad, key_heads, preferred_element_type=jnp.float32
            ) * HD ** (-0.5)
            grad_keys = jnp.einsum(
                "hqk,qhd->khd", score_grad, query_heads, preferred_element_type=jnp.float32
            ) * HD ** (-0.5)
            qkv_grad = jnp.concatenate(
                [
                    grad_query.reshape(length, width),
                    grad_keys.reshape(length, width),
                    grad_values.reshape(length, width),
                ],
                1,
            ).astype(jnp.bfloat16)
            return times_transposed(qkv_grad, qkv_full)

        def backward_ffn_case():
            act_grad = times_transposed(branch_grad, ffn_out_full)
            pre_grad = (act_grad * gelu_slope(pre_act)).astype(jnp.bfloat16)
            return times_transposed(pre_grad, ffn_in_full)

        inner = lax.cond(is_attention, backward_attention_case, backward_ffn_case)
        hidden_grad = (grad_resid + inner).astype(jnp.bfloat16)
        return (
            hidden_grad,
            (
                grad_down_matrix,
                grad_down_shift,
                grad_lift_matrix,
                grad_lift_shift,
                grad_gain,
                grad_shift,
            ),
        )

    def attention_side():
        gathered = (
            lax.all_gather(pick(qkv_weight), "dp", axis=0, tiled=True),
            lax.all_gather(pick(attn_out_weight), "dp", axis=0, tiled=True),
        )
        return (
            gathered[0],
            gathered[1],
            jnp.zeros((width, ffn_width), jnp.bfloat16),
            jnp.zeros((ffn_width, width), jnp.bfloat16),
        )

    def ffn_side():
        gathered = (
            lax.all_gather(pick(ffn_in_weight), "dp", axis=0, tiled=True),
            lax.all_gather(pick(ffn_out_weight), "dp", axis=0, tiled=True),
        )
        return (
            jnp.zeros((width, 3 * width), jnp.bfloat16),
            jnp.zeros((width, width), jnp.bfloat16),
            gathered[0],
            gathered[1],
        )

    frozen = lax.cond(is_attention, attention_side, ffn_side)
    turns = micro + section_count - 1
    buffers = jax.tree.map(
        lambda member: jnp.zeros((micro,) + member.shape, member.dtype), empty_keep()
    )

    def forward_turn(turn, carry):
        incoming, outputs, kept, totals = carry
        micro_index = turn - section_index
        is_valid = (micro_index >= 0) & (micro_index < micro)
        slot_index = jnp.clip(micro_index, 0, micro - 1)
        own_rows = lax.dynamic_index_in_dim(inputs, slot_index, 0, keepdims=False)
        hidden = jnp.where(section_index == 0, own_rows, incoming)
        allowed, valid_row = masks(slot_index)
        output, keep, square_sums = lax.cond(
            is_valid,
            lambda: forward_step(frozen, hidden, allowed, valid_row),
            lambda: (
                jnp.zeros((length, width), jnp.bfloat16),
                empty_keep(),
                jnp.zeros((2,), jnp.float32),
            ),
        )
        outputs = store(outputs, slot_index, output, is_valid)
        kept = jax.tree.map(
            lambda buffer, fresh: store(buffer, slot_index, fresh, is_valid), kept, keep
        )
        incoming = from_behind(output, "section", 1)
        return (incoming, outputs, kept, totals + square_sums)

    forward_init = (
        jnp.zeros((length, width), jnp.bfloat16),
        jnp.zeros((micro, length, width), jnp.bfloat16),
        buffers,
        jnp.zeros((2,), jnp.float32),
    )
    incoming, outputs, kept, totals = lax.fori_loop(0, turns, forward_turn, forward_init)
    zero_grads = jax.tree.map(lambda member: jnp.zeros(member.shape, jnp.float32), adapter)

    def backward_turn(turn, carry):
        incoming, input_grads, grads = carry
        micro_index = turn - (section_count - 1 - section_index)
        is_valid = (micro_index >= 0) & (micro_index < micro)
        slot_index = jnp.clip(micro_index, 0, micro - 1)
        own_rows = lax.dynamic_index_in_dim(cotangent, slot_index, 0, keepdims=False)
        grad_out = jnp.where(section_index == section_count - 1, own_rows, incoming)
        allowed = masks(slot_index)[0]
        keep = jax.tree.map(
            lambda buffer: lax.dynamic_index_in_dim(buffer, slot_index, 0, keepdims=False), kept
        )
        hidden_grad, step_grads = lax.cond(
            is_valid,
            lambda: backward_step(frozen, grad_out, keep, allowed),
            lambda: (jnp.zeros((length, width), jnp.bfloat16), zero_grads),
        )
        input_grads = store(input_grads, slot_index, hidden_grad, is_valid)
        grads = jax.tree.map(lambda total_grad, fresh: total_grad + fresh, grads, step_grads)
        incoming = from_behind(hidden_grad, "section", -1)
        return (incoming, input_grads, grads)

    backward_init = (
        jnp.zeros((length, width), jnp.bfloat16),
        jnp.zeros((micro, length, width), jnp.bfloat16),
        zero_grads,
    )
    incoming, input_grads, grads = lax.fori_loop(0, turns, backward_turn, backward_init)
    summed_all = lax.psum(
        (grads[0], grads[1], grads[2], grads[3], grads[4], grads[5], totals), "dp"
    )
    summed = summed_all[:6]
    totals = summed_all[6]
    ratios = jnp.sqrt(totals[0] / totals[1])[None]
    return (
        outputs[None],
        input_grads[None],
        summed[0][None],
        summed[1][None],
        summed[2][None],
        summed[3][None],
        summed[4][None],
        summed[5][None],
        ratios,
    )


def solution(mesh):
    in_specs = (
        P("dp", None, None),
        P("dp"),
        P("dp", None),
        P("dp", None, None),
        P("section", None, None),
        P("section", None),
        P("section", None, None),
        P("section", None),
        P("section", None),
        P("section", None),
        P(None, "dp", None),
        P(),
        P(),
        P(None, "dp", None),
        P(),
        P(None, "dp", None),
        P(),
        P(None, "dp", None),
        P(),
    )
    out_specs = (
        P("section", "dp", None, None),
        P("section", "dp", None, None),
        P("section", None, None),
        P("section", None),
        P("section", None, None),
        P("section", None),
        P("section", None),
        P("section", None),
        P("section"),
    )
    return jax.shard_map(
        on_device, mesh=mesh, in_specs=in_specs, out_specs=out_specs, check_vma=False
    )
```

profile of v0, /device:TPU:0, one launch (start us, length us, event | category | flops | bytes accessed | tf_op | source)
XLA Modules:
  0.0 1701.7 jit_solution(14286084874636791560)
XLA Ops:
  11.8 105.2 %conditional.5 = (bf16[768,2304]{1,0:T(8,128)(2,1)}, bf16[768,768]{1,0:T(8,128)(2,1)}, bf16[768,3072]{1,0:T(8,128)(2,1)}, bf16[3072,768]{1,0:T(8,128)(2,1)}) conditional(s32[]{:T(128)} %convert_element_type.221, (s32[]{:T(128)}, bf16[2,96,3072]{2,1,0:T(8,128)(2,1)S(1)}, bf16[2,384,768]{2,1,0:T(8,128)(2,1)S(1)}) %tuple.319, (s32[]{:T(128)}, ...), branch_computations={%region_0.1_spmd, %region_1.2_spmd} | conditional | flops 3 | bytes 38928544 | solution.py:308
  14.4 25.9 %all-gather.15.cloned.1.call-done = bf16[1,768,768]{2,1,0:T(8,128)(2,1)} async-done(((bf16[1,96,768]{2,1,0:T(8,128)(2,1)}), bf16[1,768,768]{2,1,0:T(8,128)(2,1)}) %all-gather.15.cloned.1.call-update) | async-done | bytes 1179664 | tf_op jit(solution)/shard_map/cond/branch_1_fun/all_gather | solution.py:287
  40.3 71.6 %all-gather.13.cloned.1.call-done = bf16[1,768,2304]{2,1,0:T(8,128)(2,1)} async-done(((bf16[1,96,2304]{2,1,0:T(8,128)(2,1)}), bf16[1,768,2304]{2,1,0:T(8,128)(2,1)}) %all-gather.13.cloned.1.call-update) | async-done | bytes 3538960 | tf_op jit(solution)/shard_map/cond/branch_1_fun/all_gather | solution.py:286
  145.5 803.5 %while.64 = (s32[]{:T(128)}, bf16[512,768]{1,0:T(8,128)(2,1)}, bf16[6,512,768]{2,1,0:T(8,128)(2,1)}, bf16[6,512,2304]{1,2,0:T(8,128)(2,1)}, f32[6,12,512]{2,1,0:...) while((s32[]{:T(128)}, bf16[512,768]{1,0:T(8,128)(2,1)}, ...), condition=%wide.region_15.16_spmd.clone, body=%wide.region_2.15_spmd.clone.sunk | while | flops 5050703872 | bytes 258192816 | solution.py:344
  164.5 51.6 %conditional.10 = (bf16[512,768]{1,0:T(8,128)(2,1)}, bf16[512,2304]{1,0:T(8,128)(2,1)}, f32[12,512]{1,0:T(8,128)}, f32[512,3072]{1,0:T(8,128)}, f32[512,768]{1,0...) conditional(s32[]{:T(128)} %convert_element_type.306, () %tuple.266, (pred[]{:T(512)}, ...), branch_computations={%region_3.3_spmd, %region_4.14_spmd} | conditional | flops 5046732800 | bytes 158299824 | solution.py:322
  167.5 36.2 %conditional = (f32[512,768]{1,0:T(8,128)}, bf16[512,2304]{1,0:T(8,128)(2,1)}, f32[12,512]{1,0:T(8,128)}, f32[512,3072]{1,0:T(8,128)}) conditional(s32[]{:T(128)} %convert_element_type.197, (bf16[512,768]{1,0:T(8,128)(2,1)}, bf16[768,3072]{1,0:T(8,128)(2,1)}, f32[3072]{0:T(1024)S(1)}, bf16[3072,768]{1,0:T(8,128)(2,1)}, ...), branch_computations={%region_5.4_spmd, %region_6.7_spmd.clone} | conditional | flops 4936040448 | bytes 145981600 | solution.py:185
  262.4 51.6 %conditional.10 = (bf16[512,768]{1,0:T(8,128)(2,1)}, bf16[512,2304]{1,0:T(8,128)(2,1)}, f32[12,512]{1,0:T(8,128)}, f32[512,3072]{1,0:T(8,128)}, f32[512,768]{1,0...) conditional(s32[]{:T(128)} %convert_element_type.306, () %tuple.266, (pred[]{:T(512)}, ...), branch_computations={%region_3.3_spmd, %region_4.14_spmd} | conditional | flops 5046732800 | bytes 158299824 | solution.py:322
  265.5 36.2 %conditional = (f32[512,768]{1,0:T(8,128)}, bf16[512,2304]{1,0:T(8,128)(2,1)}, f32[12,512]{1,0:T(8,128)}, f32[512,3072]{1,0:T(8,128)}) conditional(s32[]{:T(128)} %convert_element_type.197, (bf16[512,768]{1,0:T(8,128)(2,1)}, bf16[768,3072]{1,0:T(8,128)(2,1)}, f32[3072]{0:T(1024)S(1)}, bf16[3072,768]{1,0:T(8,128)(2,1)}, ...), branch_computations={%region_5.4_spmd, %region_6.7_spmd.clone} | conditional | flops 4936040448 | bytes 145981600 | solution.py:185
  360.5 51.6 %conditional.10 = (bf16[512,768]{1,0:T(8,128)(2,1)}, bf16[512,2304]{1,0:T(8,128)(2,1)}, f32[12,512]{1,0:T(8,128)}, f32[512,3072]{1,0:T(8,128)}, f32[512,768]{1,0...) conditional(s32[]{:T(128)} %convert_element_type.306, () %tuple.266, (pred[]{:T(512)}, ...), branch_computations={%region_3.3_spmd, %region_4.14_spmd} | conditional | flops 5046732800 | bytes 158299824 | solution.py:322
  363.6 36.2 %conditional = (f32[512,768]{1,0:T(8,128)}, bf16[512,2304]{1,0:T(8,128)(2,1)}, f32[12,512]{1,0:T(8,128)}, f32[512,3072]{1,0:T(8,128)}) conditional(s32[]{:T(128)} %convert_element_type.197, (bf16[512,768]{1,0:T(8,128)(2,1)}, bf16[768,3072]{1,0:T(8,128)(2,1)}, f32[3072]{0:T(1024)S(1)}, bf16[3072,768]{1,0:T(8,128)(2,1)}, ...), branch_computations={%region_5.4_spmd, %region_6.7_spmd.clone} | conditional | flops 4936040448 | bytes 145981600 | solution.py:185
  458.5 51.6 %conditional.10 = (bf16[512,768]{1,0:T(8,128)(2,1)}, bf16[512,2304]{1,0:T(8,128)(2,1)}, f32[12,512]{1,0:T(8,128)}, f32[512,3072]{1,0:T(8,128)}, f32[512,768]{1,0...) conditional(s32[]{:T(128)} %convert_element_type.306, () %tuple.266, (pred[]{:T(512)}, ...), branch_computations={%region_3.3_spmd, %region_4.14_spmd} | conditional | flops 5046732800 | bytes 158299824 | solution.py:322
  461.6 36.2 %conditional = (f32[512,768]{1,0:T(8,128)}, bf16[512,2304]{1,0:T(8,128)(2,1)}, f32[12,512]{1,0:T(8,128)}, f32[512,3072]{1,0:T(8,128)}) conditional(s32[]{:T(128)} %convert_element_type.197, (bf16[512,768]{1,0:T(8,128)(2,1)}, bf16[768,3072]{1,0:T(8,128)(2,1)}, f32[3072]{0:T(1024)S(1)}, bf16[3072,768]{1,0:T(8,128)(2,1)}, ...), branch_computations={%region_5.4_spmd, %region_6.7_spmd.clone} | conditional | flops 4936040448 | bytes 145981600 | solution.py:185
  556.5 51.6 %conditional.10 = (bf16[512,768]{1,0:T(8,128)(2,1)}, bf16[512,2304]{1,0:T(8,128)(2,1)}, f32[12,512]{1,0:T(8,128)}, f32[512,3072]{1,0:T(8,128)}, f32[512,768]{1,0...) conditional(s32[]{:T(128)} %convert_element_type.306, () %tuple.266, (pred[]{:T(512)}, ...), branch_computations={%region_3.3_spmd, %region_4.14_spmd} | conditional | flops 5046732800 | bytes 158299824 | solution.py:322
  559.6 36.2 %conditional = (f32[512,768]{1,0:T(8,128)}, bf16[512,2304]{1,0:T(8,128)(2,1)}, f32[12,512]{1,0:T(8,128)}, f32[512,3072]{1,0:T(8,128)}) conditional(s32[]{:T(128)} %convert_element_type.197, (bf16[512,768]{1,0:T(8,128)(2,1)}, bf16[768,3072]{1,0:T(8,128)(2,1)}, f32[3072]{0:T(1024)S(1)}, bf16[3072,768]{1,0:T(8,128)(2,1)}, ...), branch_computations={%region_5.4_spmd, %region_6.7_spmd.clone} | conditional | flops 4936040448 | bytes 145981600 | solution.py:185
  654.6 51.6 %conditional.10 = (bf16[512,768]{1,0:T(8,128)(2,1)}, bf16[512,2304]{1,0:T(8,128)(2,1)}, f32[12,512]{1,0:T(8,128)}, f32[512,3072]{1,0:T(8,128)}, f32[512,768]{1,0...) conditional(s32[]{:T(128)} %convert_element_type.306, () %tuple.266, (pred[]{:T(512)}, ...), branch_computations={%region_3.3_spmd, %region_4.14_spmd} | conditional | flops 5046732800 | bytes 158299824 | solution.py:322
  657.6 36.2 %conditional = (f32[512,768]{1,0:T(8,128)}, bf16[512,2304]{1,0:T(8,128)(2,1)}, f32[12,512]{1,0:T(8,128)}, f32[512,3072]{1,0:T(8,128)}) conditional(s32[]{:T(128)} %convert_element_type.197, (bf16[512,768]{1,0:T(8,128)(2,1)}, bf16[768,3072]{1,0:T(8,128)(2,1)}, f32[3072]{0:T(1024)S(1)}, bf16[3072,768]{1,0:T(8,128)(2,1)}, ...), branch_computations={%region_5.4_spmd, %region_6.7_spmd.clone} | conditional | flops 4936040448 | bytes 145981600 | solution.py:185
  952.5 684.1 %while.65 = (s32[]{:T(128)}, bf16[512,768]{1,0:T(8,128)(2,1)}, bf16[6,512,768]{2,1,0:T(8,128)(2,1)}, f32[768,64]{0,1:T(8,128)}, f32[64]{0:T(128)}, /*index=5*/f3...) while((s32[]{:T(128)}, bf16[512,768]{1,0:T(8,128)(2,1)}, ...), condition=%wide.region_30.31_spmd.clone, body=%wide.region_16.30_spmd.clone.sunk | while | flops 5064591872 | bytes 206468800 | solution.py:373
  1022.1 128.9 %collective-permute-done.1 = bf16[512,768]{1,0:T(8,128)(2,1)} collective-permute-done((bf16[512,768]{1,0:T(8,128)(2,1)}, bf16[512,768]{1,0:T(8,128)(2,1)}, u32[]{:S(2)}, u32[]{:S(2)}) %collective-permute-start.1) | collective-permute-done | bytes 786464 | tf_op jit(solution)/shard_map/while/body/eval_jaxpr/ppermute | solution.py:18
  1151.0 64.8 %conditional.11 = (bf16[512,768]{1,0:T(8,128)(2,1)}, f32[768,64]{0,1:T(8,128)}, f32[64]{0:T(128)S(1)}, f32[64,768]{1,0:T(8,128)}, f32[768]{0:T(1024)S(1)}, /*index=5*/f32[768]{0:T(1024)S(1)}, f32[768]{0:T(1024)S(1)}) conditional(s32[]{:T(128)} %convert_element_type.307, () %tuple.270, (f32[6,512,768]{2,1,0:T(8,128)}, s32[]{:T(128)}, pred[]{:T(512)}, ...), branch_computations={%region_17.17_spmd, %region_18.29_spmd} | conditional | flops 5063997440 | bytes 197391136 | solution.py:358
  1162.3 48.3 %conditional.2 = (f32[512,768]{1,0:T(8,128)S(1)}) conditional(s32[]{:T(128)} %convert_element_type.209, (bf16[512,768]{1,0:T(8,128)(2,1)}, bf16[3072,768]{1,0:T(8,128)(2,1)}, f32[6,512,3072]{2,1,0:T(8,128)}, s32[]{:T(128)}, bf16[768,3072]{1,0:T(8,128)(2,1)}) %tuple.173, (s32[512,1]{0,1:T(1,128)S(1)}, s32[512,1]{0,1:T(1,128)S(1)}, ...), branch_computations={%region_23.22_spmd, %region_24.24_spmd.clone} | conditional | flops 4847566848 | bytes 175045920 | solution.py:270
  1234.1 64.8 %conditional.11 = (bf16[512,768]{1,0:T(8,128)(2,1)}, f32[768,64]{0,1:T(8,128)}, f32[64]{0:T(128)S(1)}, f32[64,768]{1,0:T(8,128)}, f32[768]{0:T(1024)S(1)}, /*index=5*/f32[768]{0:T(1024)S(1)}, f32[768]{0:T(1024)S(1)}) conditional(s32[]{:T(128)} %convert_element_type.307, () %tuple.270, (f32[6,512,768]{2,1,0:T(8,128)}, s32[]{:T(128)}, pred[]{:T(512)}, ...), branch_computations={%region_17.17_spmd, %region_18.29_spmd} | conditional | flops 5063997440 | bytes 197391136 | solution.py:358
  1245.4 48.3 %conditional.2 = (f32[512,768]{1,0:T(8,128)S(1)}) conditional(s32[]{:T(128)} %convert_element_type.209, (bf16[512,768]{1,0:T(8,128)(2,1)}, bf16[3072,768]{1,0:T(8,128)(2,1)}, f32[6,512,3072]{2,1,0:T(8,128)}, s32[]{:T(128)}, bf16[768,3072]{1,0:T(8,128)(2,1)}) %tuple.173, (s32[512,1]{0,1:T(1,128)S(1)}, s32[512,1]{0,1:T(1,128)S(1)}, ...), branch_computations={%region_23.22_spmd, %region_24.24_spmd.clone} | conditional | flops 4847566848 | bytes 175045920 | solution.py:270
  1316.4 64.8 %conditional.11 = (bf16[512,768]{1,0:T(8,128)(2,1)}, f32[768,64]{0,1:T(8,128)}, f32[64]{0:T(128)S(1)}, f32[64,768]{1,0:T(8,128)}, f32[768]{0:T(1024)S(1)}, /*index=5*/f32[768]{0:T(1024)S(1)}, f32[768]{0:T(1024)S(1)}) conditional(s32[]{:T(128)} %convert_element_type.307, () %tuple.270, (f32[6,512,768]{2,1,0:T(8,128)}, s32[]{:T(128)}, pred[]{:T(512)}, ...), branch_computations={%region_17.17_spmd, %region_18.29_spmd} | conditional | flops 5063997440 | bytes 197391136 | solution.py:358
  1327.6 48.3 %conditional.2 = (f32[512,768]{1,0:T(8,128)S(1)}) conditional(s32[]{:T(128)} %convert_element_type.209, (bf16[512,768]{1,0:T(8,128)(2,1)}, bf16[3072,768]{1,0:T(8,128)(2,1)}, f32[6,512,3072]{2,1,0:T(8,128)}, s32[]{:T(128)}, bf16[768,3072]{1,0:T(8,128)(2,1)}) %tuple.173, (s32[512,1]{0,1:T(1,128)S(1)}, s32[512,1]{0,1:T(1,128)S(1)}, ...), branch_computations={%region_23.22_spmd, %region_24.24_spmd.clone} | conditional | flops 4847566848 | bytes 175045920 | solution.py:270
  1397.7 64.8 %conditional.11 = (bf16[512,768]{1,0:T(8,128)(2,1)}, f32[768,64]{0,1:T(8,128)}, f32[64]{0:T(128)S(1)}, f32[64,768]{1,0:T(8,128)}, f32[768]{0:T(1024)S(1)}, /*index=5*/f32[768]{0:T(1024)S(1)}, f32[768]{0:T(1024)S(1)}) conditional(s32[]{:T(128)} %convert_element_type.307, () %tuple.270, (f32[6,512,768]{2,1,0:T(8,128)}, s32[]{:T(128)}, pred[]{:T(512)}, ...), branch_computations={%region_17.17_spmd, %region_18.29_spmd} | conditional | flops 5063997440 | bytes 197391136 | solution.py:358
  1409.0 48.3 %conditional.2 = (f32[512,768]{1,0:T(8,128)S(1)}) conditional(s32[]{:T(128)} %convert_element_type.209, (bf16[512,768]{1,0:T(8,128)(2,1)}, bf16[3072,768]{1,0:T(8,128)(2,1)}, f32[6,512,3072]{2,1,0:T(8,128)}, s32[]{:T(128)}, bf16[768,3072]{1,0:T(8,128)(2,1)}) %tuple.173, (s32[512,1]{0,1:T(1,128)S(1)}, s32[512,1]{0,1:T(1,128)S(1)}, ...), branch_computations={%region_23.22_spmd, %region_24.24_spmd.clone} | conditional | flops 4847566848 | bytes 175045920 | solution.py:270
  1478.1 64.8 %conditional.11 = (bf16[512,768]{1,0:T(8,128)(2,1)}, f32[768,64]{0,1:T(8,128)}, f32[64]{0:T(128)S(1)}, f32[64,768]{1,0:T(8,128)}, f32[768]{0:T(1024)S(1)}, /*index=5*/f32[768]{0:T(1024)S(1)}, f32[768]{0:T(1024)S(1)}) conditional(s32[]{:T(128)} %convert_element_type.307, () %tuple.270, (f32[6,512,768]{2,1,0:T(8,128)}, s32[]{:T(128)}, pred[]{:T(512)}, ...), branch_computations={%region_17.17_spmd, %region_18.29_spmd} | conditional | flops 5063997440 | bytes 197391136 | solution.py:358
  1489.3 48.3 %conditional.2 = (f32[512,768]{1,0:T(8,128)S(1)}) conditional(s32[]{:T(128)} %convert_element_type.209, (bf16[512,768]{1,0:T(8,128)(2,1)}, bf16[3072,768]{1,0:T(8,128)(2,1)}, f32[6,512,3072]{2,1,0:T(8,128)}, s32[]{:T(128)}, bf16[768,3072]{1,0:T(8,128)(2,1)}) %tuple.173, (s32[512,1]{0,1:T(1,128)S(1)}, s32[512,1]{0,1:T(1,128)S(1)}, ...), branch_computations={%region_23.22_spmd, %region_24.24_spmd.clone} | conditional | flops 4847566848 | bytes 175045920 | solution.py:270
  1557.5 64.8 %conditional.11 = (bf16[512,768]{1,0:T(8,128)(2,1)}, f32[768,64]{0,1:T(8,128)}, f32[64]{0:T(128)S(1)}, f32[64,768]{1,0:T(8,128)}, f32[768]{0:T(1024)S(1)}, /*index=5*/f32[768]{0:T(1024)S(1)}, f32[768]{0:T(1024)S(1)}) conditional(s32[]{:T(128)} %convert_element_type.307, () %tuple.270, (f32[6,512,768]{2,1,0:T(8,128)}, s32[]{:T(128)}, pred[]{:T(512)}, ...), branch_computations={%region_17.17_spmd, %region_18.29_spmd} | conditional | flops 5063997440 | bytes 197391136 | solution.py:358
  1568.8 48.3 %conditional.2 = (f32[512,768]{1,0:T(8,128)S(1)}) conditional(s32[]{:T(128)} %convert_element_type.209, (bf16[512,768]{1,0:T(8,128)(2,1)}, bf16[3072,768]{1,0:T(8,128)(2,1)}, f32[6,512,3072]{2,1,0:T(8,128)}, s32[]{:T(128)}, bf16[768,3072]{1,0:T(8,128)(2,1)}) %tuple.173, (s32[512,1]{0,1:T(1,128)S(1)}, s32[512,1]{0,1:T(1,128)S(1)}, ...), branch_computations={%region_23.22_spmd, %region_24.24_spmd.clone} | conditional | flops 4847566848 | bytes 175045920 | solution.py:270
  1636.7 26.1 %all-reduce = (f32[1,64]{1,0:T(1,128)}, f32[1,768]{1,0:T(1,128)}, f32[1,768]{1,0:T(1,128)}, f32[1,768]{1,0:T(1,128)}, f32[2]{0:T(128)S(1)}) all-reduce(f32[1,64]{1,0:T(1,128)} %bitcast.261, f32[1,768]{1,0:T(1,128)S(1)} %broadcast_in_dim.224, f32[1,768]{1,0:T(1,128)S(1)} %broadcast_in_dim.225, ...), channel_id=1, replica_groups=mesh['section'=4,'dp'=8] {'dp'}, use_global_device_ids=true, to_apply=%region_32.33 | all-reduce | flops 2370 | bytes 18960 | tf_op jit(solution)/shard_map/psum | solution.py:374
  1664.8 24.9 %all-reduce.4.cloned.1.call-done = (f32[1,768,64]{1,2,0:T(8,128)}, f32[1,64,768]{2,1,0:T(8,128)}) async-done(((f32[1,768,64]{1,2,0:T(8,128)}, f32[1,64,768]{2,1,0:T(8,128)}), (f32[1,768,64]{1,2,0:T(8,128)}, f32[1,64,768]{2,1,0:T(8,128)})) %all-reduce.4.cloned.1.call-update) | async-done | bytes 393232 | tf_op jit(solution)/shard_map/psum | solution.py:374
  (1000 shorter events, 1398.4 us)
Async XLA Ops:
  11.8 28.4 %all-gather.15.cloned.1.call-start = ((), (), s32[]{:S(2)}) async-start(), calls=%async_computation.3 | async-start | bytes 1327104 | tf_op jit(solution)/shard_map/cond/branch_1_fun/all_gather | solution.py:287
  13.5 98.4 %all-gather.13.cloned.1.call-start = ((), (), s32[]{:S(2)}) async-start(), calls=%async_computation.2 | async-start | bytes 3981312 | tf_op jit(solution)/shard_map/cond/branch_1_fun/all_gather | solution.py:286
  117.1 1572.6 %all-reduce.4.cloned.1.call-start = ((), (), s32[]{:S(2)}) async-start(), calls=%async_computation.4 | async-start | bytes 786432 | tf_op jit(solution)/shard_map/psum | solution.py:374
  216.0 46.4 %collective-permute-start = (bf16[512,768]{1,0:T(8,128)(2,1)}, bf16[512,768]{1,0:T(8,128)(2,1)}, u32[]{:S(2)}, u32[]{:S(2)}) collective-permute-start(bf16[512,768]{1,0:T(8,128)(2,1)} %get-tuple-element.3866), channel_id=1, source_target_pairs={{0,8},{8,16},{16,24},{1,9},{9,17},{17,25},{2,10},{10,18},{18,26},{... | collective-permute-start | bytes 2359304 | tf_op jit(solution)/shard_map/while/body/eval_jaxpr/ppermute | solution.py:18
  314.0 46.5 %collective-permute-start = (bf16[512,768]{1,0:T(8,128)(2,1)}, bf16[512,768]{1,0:T(8,128)(2,1)}, u32[]{:S(2)}, u32[]{:S(2)}) collective-permute-start(bf16[512,768]{1,0:T(8,128)(2,1)} %get-tuple-element.3866), channel_id=1, source_target_pairs={{0,8},{8,16},{16,24},{1,9},{9,17},{17,25},{2,10},{10,18},{18,26},{... | collective-permute-start | bytes 2359304 | tf_op jit(solution)/shard_map/while/body/eval_jaxpr/ppermute | solution.py:18
  412.1 46.4 %collective-permute-start = (bf16[512,768]{1,0:T(8,128)(2,1)}, bf16[512,768]{1,0:T(8,128)(2,1)}, u32[]{:S(2)}, u32[]{:S(2)}) collective-permute-start(bf16[512,768]{1,0:T(8,128)(2,1)} %get-tuple-element.3866), channel_id=1, source_target_pairs={{0,8},{8,16},{16,24},{1,9},{9,17},{17,25},{2,10},{10,18},{18,26},{... | collective-permute-start | bytes 2359304 | tf_op jit(solution)/shard_map/while/body/eval_jaxpr/ppermute | solution.py:18
  510.1 46.4 %collective-permute-start = (bf16[512,768]{1,0:T(8,128)(2,1)}, bf16[512,768]{1,0:T(8,128)(2,1)}, u32[]{:S(2)}, u32[]{:S(2)}) collective-permute-start(bf16[512,768]{1,0:T(8,128)(2,1)} %get-tuple-element.3866), channel_id=1, source_target_pairs={{0,8},{8,16},{16,24},{1,9},{9,17},{17,25},{2,10},{10,18},{18,26},{... | collective-permute-start | bytes 2359304 | tf_op jit(solution)/shard_map/while/body/eval_jaxpr/ppermute | solution.py:18
  608.1 46.5 %collective-permute-start = (bf16[512,768]{1,0:T(8,128)(2,1)}, bf16[512,768]{1,0:T(8,128)(2,1)}, u32[]{:S(2)}, u32[]{:S(2)}) collective-permute-start(bf16[512,768]{1,0:T(8,128)(2,1)} %get-tuple-element.3866), channel_id=1, source_target_pairs={{0,8},{8,16},{16,24},{1,9},{9,17},{17,25},{2,10},{10,18},{18,26},{... | collective-permute-start | bytes 2359304 | tf_op jit(solution)/shard_map/while/body/eval_jaxpr/ppermute | solution.py:18
  706.2 46.5 %collective-permute-start = (bf16[512,768]{1,0:T(8,128)(2,1)}, bf16[512,768]{1,0:T(8,128)(2,1)}, u32[]{:S(2)}, u32[]{:S(2)}) collective-permute-start(bf16[512,768]{1,0:T(8,128)(2,1)} %get-tuple-element.3866), channel_id=1, source_target_pairs={{0,8},{8,16},{16,24},{1,9},{9,17},{17,25},{2,10},{10,18},{18,26},{... | collective-permute-start | bytes 2359304 | tf_op jit(solution)/shard_map/while/body/eval_jaxpr/ppermute | solution.py:18
  762.4 49.8 %collective-permute-start = (bf16[512,768]{1,0:T(8,128)(2,1)}, bf16[512,768]{1,0:T(8,128)(2,1)}, u32[]{:S(2)}, u32[]{:S(2)}) collective-permute-start(bf16[512,768]{1,0:T(8,128)(2,1)} %get-tuple-element.3866), channel_id=1, source_target_pairs={{0,8},{8,16},{16,24},{1,9},{9,17},{17,25},{2,10},{10,18},{18,26},{... | collective-permute-start | bytes 2359304 | tf_op jit(solution)/shard_map/while/body/eval_jaxpr/ppermute | solution.py:18
  822.1 46.2 %collective-permute-start = (bf16[512,768]{1,0:T(8,128)(2,1)}, bf16[512,768]{1,0:T(8,128)(2,1)}, u32[]{:S(2)}, u32[]{:S(2)}) collective-permute-start(bf16[512,768]{1,0:T(8,128)(2,1)} %get-tuple-element.3866), channel_id=1, source_target_pairs={{0,8},{8,16},{16,24},{1,9},{9,17},{17,25},{2,10},{10,18},{18,26},{... | collective-permute-start | bytes 2359304 | tf_op jit(solution)/shard_map/while/body/eval_jaxpr/ppermute | solution.py:18
  878.1 56.5 %collective-permute-start = (bf16[512,768]{1,0:T(8,128)(2,1)}, bf16[512,768]{1,0:T(8,128)(2,1)}, u32[]{:S(2)}, u32[]{:S(2)}) collective-permute-start(bf16[512,768]{1,0:T(8,128)(2,1)} %get-tuple-element.3866), channel_id=1, source_target_pairs={{0,8},{8,16},{16,24},{1,9},{9,17},{17,25},{2,10},{10,18},{18,26},{... | collective-permute-start | bytes 2359304 | tf_op jit(solution)/shard_map/while/body/eval_jaxpr/ppermute | solution.py:18
  954.9 26.3 %copy-start.9 = (bf16[768,64]{1,0:T(8,128)(2,1)S(1)}, bf16[768,64]{1,0:T(8,128)(2,1)}, u32[]{:S(2)}) copy-start(bf16[768,64]{1,0:T(8,128)(2,1)} %get-tuple-element.4211) | copy-start | bytes 294916 | tf_op jit(solution)/shard_map/while
  954.9 26.3 %copy-start.12 = (bf16[64,768]{1,0:T(8,128)(2,1)S(1)}, bf16[64,768]{1,0:T(8,128)(2,1)}, u32[]{:S(2)}) copy-start(bf16[64,768]{1,0:T(8,128)(2,1)} %get-tuple-element.4249) | copy-start | bytes 294916 | tf_op jit(solution)/shard_map/while
  955.0 26.3 %collective-permute-start.1 = (bf16[512,768]{1,0:T(8,128)(2,1)}, bf16[512,768]{1,0:T(8,128)(2,1)}, u32[]{:S(2)}, u32[]{:S(2)}) collective-permute-start(bf16[512,768]{1,0:T(8,128)(2,1)} %get-tuple-element.3904), channel_id=1, source_target_pairs={{8,0},{16,8},{24,16},{9,1},{17,9},{25,17},{10,2},{18,10},{26,18},{... | collective-permute-start | bytes 2359304 | tf_op jit(solution)/shard_map/while/body/eval_jaxpr/ppermute | solution.py:18
  983.6 27.7 %copy-start.9 = (bf16[768,64]{1,0:T(8,128)(2,1)S(1)}, bf16[768,64]{1,0:T(8,128)(2,1)}, u32[]{:S(2)}) copy-start(bf16[768,64]{1,0:T(8,128)(2,1)} %get-tuple-element.4211) | copy-start | bytes 294916 | tf_op jit(solution)/shard_map/while
  983.7 27.7 %copy-start.12 = (bf16[64,768]{1,0:T(8,128)(2,1)S(1)}, bf16[64,768]{1,0:T(8,128)(2,1)}, u32[]{:S(2)}) copy-start(bf16[64,768]{1,0:T(8,128)(2,1)} %get-tuple-element.4249) | copy-start | bytes 294916 | tf_op jit(solution)/shard_map/while
  983.7 27.7 %collective-permute-start.1 = (bf16[512,768]{1,0:T(8,128)(2,1)}, bf16[512,768]{1,0:T(8,128)(2,1)}, u32[]{:S(2)}, u32[]{:S(2)}) collective-permute-start(bf16[512,768]{1,0:T(8,128)(2,1)} %get-tuple-element.3904), channel_id=1, source_target_pairs={{8,0},{16,8},{24,16},{9,1},{17,9},{25,17},{10,2},{18,10},{26,18},{... | collective-permute-start | bytes 2359304 | tf_op jit(solution)/shard_map/while/body/eval_jaxpr/ppermute | solution.py:18
  1013.8 137.2 %copy-start.9 = (bf16[768,64]{1,0:T(8,128)(2,1)S(1)}, bf16[768,64]{1,0:T(8,128)(2,1)}, u32[]{:S(2)}) copy-start(bf16[768,64]{1,0:T(8,128)(2,1)} %get-tuple-element.4211) | copy-start | bytes 294916 | tf_op jit(solution)/shard_map/while
  1013.8 137.2 %copy-start.12 = (bf16[64,768]{1,0:T(8,128)(2,1)S(1)}, bf16[64,768]{1,0:T(8,128)(2,1)}, u32[]{:S(2)}) copy-start(bf16[64,768]{1,0:T(8,128)(2,1)} %get-tuple-element.4249) | copy-start | bytes 294916 | tf_op jit(solution)/shard_map/while
  1013.8 137.2 %collective-permute-start.1 = (bf16[512,768]{1,0:T(8,128)(2,1)}, bf16[512,768]{1,0:T(8,128)(2,1)}, u32[]{:S(2)}, u32[]{:S(2)}) collective-permute-start(bf16[512,768]{1,0:T(8,128)(2,1)} %get-tuple-element.3904), channel_id=1, source_target_pairs={{8,0},{16,8},{24,16},{9,1},{17,9},{25,17},{10,2},{18,10},{26,18},{... | collective-permute-start | bytes 2359304 | tf_op jit(solution)/shard_map/while/body/eval_jaxpr/ppermute | solution.py:18
  1215.7 18.4 %copy-start.9 = (bf16[768,64]{1,0:T(8,128)(2,1)S(1)}, bf16[768,64]{1,0:T(8,128)(2,1)}, u32[]{:S(2)}) copy-start(bf16[768,64]{1,0:T(8,128)(2,1)} %get-tuple-element.4211) | copy-start | bytes 294916 | tf_op jit(solution)/shard_map/while
  1215.7 18.4 %copy-start.12 = (bf16[64,768]{1,0:T(8,128)(2,1)S(1)}, bf16[64,768]{1,0:T(8,128)(2,1)}, u32[]{:S(2)}) copy-start(bf16[64,768]{1,0:T(8,128)(2,1)} %get-tuple-element.4249) | copy-start | bytes 294916 | tf_op jit(solution)/shard_map/while
  1215.8 18.4 %collective-permute-start.1 = (bf16[512,768]{1,0:T(8,128)(2,1)}, bf16[512,768]{1,0:T(8,128)(2,1)}, u32[]{:S(2)}, u32[]{:S(2)}) collective-permute-start(bf16[512,768]{1,0:T(8,128)(2,1)} %get-tuple-element.3904), channel_id=1, source_target_pairs={{8,0},{16,8},{24,16},{9,1},{17,9},{25,17},{10,2},{18,10},{26,18},{... | collective-permute-start | bytes 2359304 | tf_op jit(solution)/shard_map/while/body/eval_jaxpr/ppermute | solution.py:18
  1298.9 17.4 %copy-start.9 = (bf16[768,64]{1,0:T(8,128)(2,1)S(1)}, bf16[768,64]{1,0:T(8,128)(2,1)}, u32[]{:S(2)}) copy-start(bf16[768,64]{1,0:T(8,128)(2,1)} %get-tuple-element.4211) | copy-start | bytes 294916 | tf_op jit(solution)/shard_map/while
  1298.9 17.5 %copy-start.12 = (bf16[64,768]{1,0:T(8,128)(2,1)S(1)}, bf16[64,768]{1,0:T(8,128)(2,1)}, u32[]{:S(2)}) copy-start(bf16[64,768]{1,0:T(8,128)(2,1)} %get-tuple-element.4249) | copy-start | bytes 294916 | tf_op jit(solution)/shard_map/while
  1298.9 17.4 %collective-permute-start.1 = (bf16[512,768]{1,0:T(8,128)(2,1)}, bf16[512,768]{1,0:T(8,128)(2,1)}, u32[]{:S(2)}, u32[]{:S(2)}) collective-permute-start(bf16[512,768]{1,0:T(8,128)(2,1)} %get-tuple-element.3904), channel_id=1, source_target_pairs={{8,0},{16,8},{24,16},{9,1},{17,9},{25,17},{10,2},{18,10},{26,18},{... | collective-permute-start | bytes 2359304 | tf_op jit(solution)/shard_map/while/body/eval_jaxpr/ppermute | solution.py:18
  1381.1 16.5 collective-permute-start.1
  1462.4 15.6 collective-permute-start.1
  1542.8 14.7 collective-permute-start.1
  1622.3 14.3 collective-permute-start.1
  1636.6 56.3 %copy-start.1 = (f32[2,3072]{1,0:T(2,128)S(1)}, f32[2,3072]{1,0:T(2,128)}, u32[]{:S(2)}) copy-start(f32[2,3072]{1,0:T(2,128)} %param.49) | copy-start | bytes 73732
  (114 other events, 824.2 us)
Sparse Core Ops, SparseCore 0:
  14.9 25.3 all-gather.14
  42.5 69.3 all-gather.12
Sparse Core Ops, SparseCore 1:
  1636.7 52.9 all-reduce.3
where the time goes:
time: 1720 us; the launch traced here: 1700 us
  local copies, waits for them, and re-layouts  430 us (25%)
  other arithmetic  411 us (24%)
  matrix products  372 us (22%)
  waiting for transfers between devices  330 us (19%)
  starting transfers between devices  69.9 us (4%)
  loops' own time  43.8 us (3%)
  blocking collectives  26.1 us (2%)
  between operations  18.5 us (1%)
    ppermute x18, waiting for transfers between devices, from_behind(): lax.ppermute(value, axis, [(source, source + steps) for source in range(i...  207 us
    dynamic_slice x81, local copies, waits for them, and re-layouts, store(): previous = lax.dynamic_index_in_dim(buffer, slot_index, 0, keepdims=False)  190 us
    dynamic_update_slice x54, other arithmetic, store(): lax.dynamic_update_index_in_dim(buffer, jnp.where(is_valid, fresh, previo...  145 us
    dot_general x24, matrix products, product(): return jnp.dot(left, right, preferred_element_type=jnp.float32)  81.2 us
    all_gather x1, waiting for transfers between devices, attention_side(): lax.all_gather(pick(qkv_weight), 'dp', axis=0, tiled=True)  71.6 us
    ppermute x18, starting transfers between devices, from_behind(): lax.ppermute(value, axis, [(source, source + steps) for source in range(i...  69.8 us
    another operation x49, local copies, waits for them, and re-layouts  69.6 us
    dot_general x6, matrix products, backward_attention_case(): jnp.einsum('qhd,khd->hqk', attended_grad, value_heads, preferred_element_...  68.7 us
  transfers between devices with their start and end apart: 21, of which 12 were waited for; matrix products, arithmetic and copies ran while one was open for 26% of the time, Pallas kernels for 0%

commit v1 on v0

v1 whole, which is shorter than its diff:
```python
import functools
import jax
import jax.numpy as jnp
from jax import lax
from jax.experimental import pallas as pl
from jax.experimental.pallas import tpu as pltpu
from jax.sharding import PartitionSpec as P

HEADS = 12
HD = 64
SEG = 64
EPSILON = 1e-05
MASKED = -1e30
LOG_TOP = 24
VMEM_BYTES = 56 * 1024 * 1024
F32 = jnp.float32
BF16 = jnp.bfloat16


def dot(left, right):
    return jnp.dot(left, right, preferred_element_type=F32)


def dot_nt(left, right):
    return lax.dot_general(left, right, (((1,), (1,)), ((), ())), preferred_element_type=F32)


def dot_tn(left, right):
    return lax.dot_general(left, right, (((0,), (0,)), ((), ())), preferred_element_type=F32)


def gelu_both(v):
    bell = jnp.exp(v * v * -0.5)
    t = 1.0 / (1.0 + jnp.abs(v) * (0.3275911 * 0.7071067811865476))
    tail = t * (
        0.127414796
        + t * (-0.142248368 + t * (0.7107068705 + t * (-0.7265760135 + t * 0.5307027145)))
    )
    tail = tail * bell
    cdf = jnp.where(v >= 0, 1.0 - tail, tail)
    return (v * cdf, cdf + v * bell * 0.3989422804014327)


def lanes(rows):
    return lax.broadcasted_iota(jnp.int32, (rows, 128), 1)


def adapter_forward(hidden, branch, adapter_ref, vec_ref, base, stage, aux, valid):
    down_t = adapter_ref[0, stage, :64]
    lift = adapter_ref[0, stage, 64:]
    branch_low = branch.astype(BF16)
    down = dot_nt(branch_low, down_t) + vec_ref[0, base + 4 : base + 5, :64]
    act, _ = gelu_both(down)
    lifted = dot(act.astype(BF16), lift) + vec_ref[0, base + 1 : base + 2]
    hidden_float = hidden.astype(F32)
    resid = hidden_float + branch + lifted
    mean = jnp.mean(resid, -1, keepdims=True)
    center = resid - mean
    inverse = lax.rsqrt(jnp.mean(center * center, -1, keepdims=True) + EPSILON)
    normed = center * inverse
    output = (normed * vec_ref[0, base + 2 : base + 3] + vec_ref[0, base + 3 : base + 4]).astype(BF16)
    sums = (
        jnp.sum(lifted * lifted * valid, 0, keepdims=True),
        jnp.sum(hidden_float * hidden_float * valid, 0, keepdims=True),
    )
    return branch_low, down, output, normed.astype(BF16), inverse, sums


def column_copies(weight, kind, chunk, held, sem):
    return pltpu.make_async_copy(weight.at[:, chunk, kind], held.at[chunk], sem)


def row_copies(weight, kind, chunk, held, sem):
    span = held.shape[1]
    return pltpu.make_async_copy(weight.at[pl.ds(chunk * span, span), :, kind], held.at[chunk], sem)


def start_copies(choice, sources, order, sems):
    made = []
    for which, source in enumerate(sources):
        copies = [make(source[matrix][0], source[matrix][1], chunk, held, sems.at[i])
                  for i, (make, matrix, chunk, held) in enumerate(order)]
        made.append(copies)

        @pl.when(choice == which)
        def _():
            for copy in copies:
                copy.start()

    return made[0]


def square(held, chunk):
    width = held.shape[-1]
    return held[chunk].reshape(width, width)


def attention_pair_forward(p, start, size, qkv, keyb, att, aux):
    rows = pl.ds(start, size)
    width = att.shape[1]
    col = pl.multiple_of(p * 128, 128)
    lane = lanes(size)
    query = qkv[rows, pl.ds(col, 128)]
    key = qkv[rows, pl.ds(width + col, 128)]
    value = qkv[rows, pl.ds(2 * width + col, 128)]
    bias = keyb[rows]
    place = start + lax.broadcasted_iota(jnp.int32, (size, 128), 0)
    hot = jnp.where(lane % 64 == place // SEG, 1.0, 0.0).astype(BF16)
    query = query * jnp.asarray(HD ** -0.5, BF16)
    total = None
    for half in range(2):
        mine = (lane < 64) if half == 0 else (lane >= 64)
        scores = dot_nt(jnp.where(mine, query, hot), jnp.where(mine, key, bias))
        peak = jnp.max(scores, -1, keepdims=True)
        expo = jnp.exp(scores - peak)
        norm = jnp.sum(expo, -1, keepdims=True)
        part = dot(expo.astype(BF16), jnp.where(mine, value, jnp.zeros_like(value))) * (1.0 / norm)
        log_total = peak + jnp.log(norm)
        aux[rows] = jnp.where(lane == 80 + 2 * p + half, log_total, aux[rows])
        total = part if total is None else total + part
    att[rows, pl.ds(col, 128)] = total.astype(BF16)


def forward_kernel(
    sources, idx, hidden_ref, keyb_ref, adapter_ref, vec_ref, in_bias_ref,
    h1_ref, h2_ref, qkv_ref, att_ref, br1_ref, nh1_ref, aux1_ref, slope_ref, br2_ref, nh2_ref, aux2_ref, sums_ref,
    attn_v, in_v, out_v, acc, sems,
):
    bucket = idx[1]
    length, width = hidden_ref.shape
    chunks = in_v.shape[0]
    cols = [pl.ds(c * width, width) for c in range(chunks)]
    order = [(column_copies, 0, c, attn_v) for c in range(4)]
    for c in range(chunks):
        order.append((column_copies, 1, c, in_v))
        order.append((row_copies, 2, c, out_v))
    copies = start_copies(idx[2], sources, order, sems)
    hidden = hidden_ref[...]
    valid = keyb_ref[:, 16:17].astype(F32)
    for part in range(3):
        copies[part].wait()
        mixed = dot(hidden, square(attn_v, part))
        if part == 0:
            mixed = mixed + vec_ref[0, 5:6]
        if part == 2:
            mixed = mixed + vec_ref[0, 6:7]
        qkv_ref[:, cols[part]] = mixed.astype(BF16)
    aux1_ref[...] = jnp.zeros_like(aux1_ref)

    def heads(size):
        blocks = length // size

        def body(step, carry):
            p = step // blocks
            start = pl.multiple_of((step % blocks) * size, size)
            attention_pair_forward(p, start, size, qkv_ref, keyb_ref, att_ref, aux1_ref)
            return carry

        lax.fori_loop(0, (HEADS // 2) * blocks, body, 0)

    @pl.when(bucket >= 3)
    def _():
        heads(length)

    @pl.when(bucket < 3)
    def _():
        heads(length // 2)

    copies[3].wait()
    branch = dot(att_ref[...], square(attn_v, 3)) + vec_ref[0, 0:1]
    branch_low, down, output, normed, inverse, sums = adapter_forward(
        hidden, branch, adapter_ref, vec_ref, 0, 0, None, valid
    )
    br1_ref[...] = branch_low
    nh1_ref[...] = normed
    h1_ref[...] = output
    lane = lanes(length)
    aux1_ref[:, :64] = down
    aux1_ref[...] = jnp.where(lane == 64, inverse, aux1_ref[...])
    sums_ref[0:1] = sums[0]
    sums_ref[1:2] = sums[1]
    hidden = h1_ref[...]
    for c in range(chunks):
        copies[4 + 2 * c].wait()
        pre = dot(hidden, square(in_v, c)) + in_bias_ref[0, :, c * width : (c + 1) * width]
        act, slope = gelu_both(pre)
        slope_ref[:, cols[c]] = slope.astype(BF16)
        copies[5 + 2 * c].wait()
        term = dot(act.astype(BF16), square(out_v, c))
        if c == 0:
            acc[...] = term + vec_ref[0, 8:9]
        else:
            acc[...] += term
    branch_low, down, output, normed, inverse, sums = adapter_forward(
        hidden, acc[...], adapter_ref, vec_ref, 8, 1, None, valid
    )
    br2_ref[...] = branch_low
    nh2_ref[...] = normed
    h2_ref[...] = output
    aux2_ref[...] = jnp.where(lane == 64, inverse, jnp.zeros((length, 128), F32))
    aux2_ref[:, :64] = down
    sums_ref[2:3] = sums[0]
    sums_ref[3:4] = sums[1]
    sums_ref[4:8] = jnp.zeros_like(sums_ref[4:8])


def weight_plan(weights):
    arrays, places = [], []
    for layer in weights:
        spots = []
        for array, kind in layer:
            found = [i for i, other in enumerate(arrays) if other is array]
            if not found:
                arrays.append(array)
                found = [len(arrays) - 1]
            spots.append((found[0], kind))
        places.append(spots)
    return arrays, places


def weight_scratch(weights):
    attn, inner, outer = [array.shape for array, _ in weights[0]]
    width = attn[-1]
    span = width // (4 * outer[3])
    return [
        pltpu.VMEM((4, attn[0], attn[3], width), BF16),
        pltpu.VMEM((4, inner[0], inner[3], width), BF16),
        pltpu.VMEM((outer[0] // span, span, 4, outer[3], width), BF16),
    ]


def whole(shape):
    return pl.BlockSpec(shape, lambda i, s: (0,) * len(shape))


def by_layer(shape):
    return pl.BlockSpec((1,) + shape, lambda i, s: (s[0],) + (0,) * len(shape))


def call_with_weights(kernel, weights, blocks, outs, scratch, flops, name):
    arrays, places = weight_plan(weights)
    fixed = len(blocks)
    idx, rest = blocks[0], blocks[1:]

    def body(*refs):
        held = refs[fixed : fixed + len(arrays)]
        sources = [[(held[i], kind) for i, kind in spots] for spots in places]
        kernel(sources, *refs[:fixed], *refs[fixed + len(arrays) :])

    copies = 12
    return pl.pallas_call(
        body,
        grid_spec=pltpu.PrefetchScalarGridSpec(
            num_scalar_prefetch=1,
            grid=(1,),
            in_specs=[spec for _, spec in rest] + [pl.BlockSpec(memory_space=pl.ANY)] * len(arrays),
            out_specs=[whole(shape) for shape, _ in outs],
            scratch_shapes=weight_scratch(weights) + scratch + [pltpu.SemaphoreType.DMA((copies,))],
        ),
        out_shape=[jax.ShapeDtypeStruct(shape, dtype) for shape, dtype in outs],
        compiler_params=pltpu.CompilerParams(vmem_limit_bytes=VMEM_BYTES),
        cost_estimate=pl.CostEstimate(flops=flops, bytes_accessed=24_000_000, transcendentals=0),
        name=name,
    )(idx, *[array for array, _ in rest], *arrays)


def forward_pair(layer, choice, bucket, hidden, keyb, weights, adapters, vecs, in_bias):
    length, width = hidden.shape
    ffn = in_bias.shape[-1]
    idx = jnp.stack([layer, bucket, choice]).astype(jnp.int32)
    outs = [
        ((length, width), BF16), ((length, width), BF16), ((length, 3 * width), BF16), ((length, width), BF16),
        ((length, width), BF16), ((length, width), BF16), ((length, 128), F32), ((length, ffn), BF16),
        ((length, width), BF16), ((length, width), BF16), ((length, 128), F32), ((8, width), F32),
    ]
    blocks = [
        idx, (hidden, whole((length, width))), (keyb, whole((length, 128))), (adapters, by_layer((2, 128, width))),
        (vecs, by_layer((16, width))), (in_bias, by_layer((1, ffn))),
    ]
    scratch = [pltpu.VMEM((length, width), F32)]
    return call_with_weights(forward_kernel, weights, blocks, outs, scratch, 12_000_000_000, "forward_pair")


def adapter_backward(grad, normed, branch_low, aux, adapter_ref, vec_ref, base, stage, grads_ref):
    down_t = adapter_ref[0, stage, :64]
    lift = adapter_ref[0, stage, 64:]
    grad = grad.astype(F32)
    normed = normed.astype(F32)
    inverse = aux[:, 64:65]
    down = aux[:, :64]
    scaled = grad * vec_ref[0, base + 2 : base + 3]
    resid = inverse * (
        scaled
        - jnp.mean(scaled, -1, keepdims=True)
        - normed * jnp.mean(scaled * normed, -1, keepdims=True)
    )
    lift_grad = resid.astype(BF16)
    act, slope = gelu_both(down)
    down_grad = (dot_nt(lift_grad, lift) * slope).astype(BF16)
    grads_ref[stage, 0:64] = dot_tn(act.astype(BF16), lift_grad)
    grads_ref[stage, 64:128] = dot_tn(down_grad, branch_low)
    grads_ref[stage, 128:136] = jnp.zeros_like(grads_ref[stage, 128:136])
    grads_ref[stage, 128:129] = jnp.sum(lift_grad.astype(F32), 0, keepdims=True)
    grads_ref[stage, 129:130] = jnp.sum(normed * grad, 0, keepdims=True)
    grads_ref[stage, 130:131] = jnp.sum(grad, 0, keepdims=True)
    grads_ref[stage, 131:132, :64] = jnp.sum(down_grad.astype(F32), 0, keepdims=True)
    branch_grad = (resid + dot(down_grad, down_t)).astype(BF16)
    return resid, branch_grad


def split_low(column):
    high = column.astype(BF16).astype(F32)
    rest = column - high
    middle = rest.astype(BF16).astype(F32)
    return high, middle, rest - middle


def attention_pair_backward(p, start, size, qkv, keyb, att, aux, att_grad, dqkv):
    rows = pl.ds(start, size)
    width = att.shape[1]
    col = pl.multiple_of(p * 128, 128)
    lane = lanes(size)
    query = qkv[rows, pl.ds(col, 128)] * jnp.asarray(HD ** -0.5, BF16)
    key = qkv[rows, pl.ds(width + col, 128)]
    value = qkv[rows, pl.ds(2 * width + col, 128)]
    grad = att_grad[rows, pl.ds(col, 128)]
    product = grad.astype(F32) * att[rows, pl.ds(col, 128)].astype(F32)
    bias = keyb[rows]
    place = start + lax.broadcasted_iota(jnp.int32, (size, 128), 0)
    spot = lane % 64
    hot = jnp.where(spot == place // SEG, 1.0, 0.0)
    aux_rows = aux[rows]
    zero = jnp.zeros((size, 128), BF16)
    sums = [None, None, None]
    for half in range(2):
        mine = (lane < 64) if half == 0 else (lane >= 64)
        log_total = jnp.sum(jnp.where(lane == 80 + 2 * p + half, aux_rows, 0.0), -1, keepdims=True)
        parts = split_low(-log_total)
        extra = jnp.where(spot == LOG_TOP, parts[0], jnp.where(spot == LOG_TOP + 1, parts[1], jnp.where(spot == LOG_TOP + 2, parts[2], hot)))
        row_dot = jnp.sum(jnp.where(mine, product, 0.0), -1, keepdims=True)
        dots = split_low(-row_dot)
        extra_grad = jnp.where(spot == LOG_TOP, dots[0], jnp.where(spot == LOG_TOP + 1, dots[1], jnp.where(spot == LOG_TOP + 2, dots[2], 0.0)))
        key_side = jnp.where(mine, key, bias)
        value_side = jnp.where(mine, value, bias)
        probs = jnp.exp(dot_nt(key_side, jnp.where(mine, query, extra.astype(BF16))))
        centred = dot_nt(value_side, jnp.where(mine, grad, extra_grad.astype(BF16)))
        score_grad = (probs * centred).astype(BF16)
        terms = (
            dot_tn(score_grad, jnp.where(mine, key, zero)),
            dot(score_grad, jnp.where(mine, query, zero)),
            dot(probs.astype(BF16), jnp.where(mine, grad, zero)),
        )
        sums = [t if s is None else s + t for s, t in zip(sums, terms)]
    dqkv[rows, pl.ds(col, 128)] = (sums[0] * HD ** -0.5).astype(BF16)
    dqkv[rows, pl.ds(width + col, 128)] = sums[1].astype(BF16)
    dqkv[rows, pl.ds(2 * width + col, 128)] = sums[2].astype(BF16)


def backward_kernel(
    sources, idx, grad_ref, keyb_ref, qkv_ref, att_ref, br1_ref, nh1_ref, aux1_ref, slope_ref, br2_ref, nh2_ref,
    aux2_ref, adapter_ref, vec_ref,
    g2_ref, g1_ref, grads_ref,
    attn_v, in_v, out_v, acc, low, dqkv, sems,
):
    bucket = idx[1]
    length, width = grad_ref.shape
    chunks = in_v.shape[0]
    cols = [pl.ds(c * width, width) for c in range(chunks)]
    order = []
    for c in range(chunks):
        order.append((row_copies, 2, c, out_v))
        order.append((column_copies, 1, c, in_v))
    order += [(column_copies, 0, c, attn_v) for c in (3, 0, 1, 2)]
    copies = start_copies(idx[2], sources, order, sems)
    resid, branch_grad = adapter_backward(
        grad_ref[...], nh2_ref[...], br2_ref[...], aux2_ref[...], adapter_ref, vec_ref, 8, 1, grads_ref
    )
    acc[...] = resid
    low[...] = branch_grad
    for c in range(chunks):
        copies[2 * c].wait()
        act_grad = dot_nt(low[...], square(out_v, c))
        pre_grad = (act_grad * slope_ref[:, cols[c]].astype(F32)).astype(BF16)
        copies[2 * c + 1].wait()
        acc[...] += dot_nt(pre_grad, square(in_v, c))
    g2_ref[...] = acc[...].astype(BF16)
    resid, branch_grad = adapter_backward(
        g2_ref[...], nh1_ref[...], br1_ref[...], aux1_ref[...], adapter_ref, vec_ref, 0, 0, grads_ref
    )
    acc[...] = resid
    copies[2 * chunks].wait()
    low[...] = dot_nt(branch_grad, square(attn_v, 3)).astype(BF16)

    def heads(size):
        blocks = length // size

        def body(step, carry):
            p = step // blocks
            start = pl.multiple_of((step % blocks) * size, size)
            attention_pair_backward(p, start, size, qkv_ref, keyb_ref, att_ref, aux1_ref, low, dqkv)
            return carry

        lax.fori_loop(0, (HEADS // 2) * blocks, body, 0)

    @pl.when(bucket >= 3)
    def _():
        heads(length)

    @pl.when(bucket < 3)
    def _():
        heads(length // 2)

    for part in range(3):
        copies[2 * chunks + 1 + part].wait()
        acc[...] += dot_nt(dqkv[:, cols[part]], square(attn_v, part))
    g1_ref[...] = acc[...].astype(BF16)


def backward_pair(layer, choice, bucket, grad, keyb, saved, weights, adapters, vecs):
    length, width = grad.shape
    idx = jnp.stack([layer, bucket, choice]).astype(jnp.int32)
    outs = [((length, width), BF16), ((length, width), BF16), ((2, 136, width), F32)]
    blocks = [idx, (grad, whole((length, width))), (keyb, whole((length, 128)))]
    blocks += [(member, whole(member.shape)) for member in saved]
    blocks += [(adapters, by_layer((2, 128, width))), (vecs, by_layer((16, width)))]
    scratch = [
        pltpu.VMEM((length, width), F32),
        pltpu.VMEM((length, width), BF16),
        pltpu.VMEM((length, 3 * width), BF16),
    ]
    return call_with_weights(backward_kernel, weights, blocks, outs, scratch, 16_000_000_000, "backward_pair")


def key_table(bucket, padding):
    rows, length = padding.shape
    spot = jnp.arange(128, dtype=jnp.int32) % 64
    shift = 6 + bucket[:, None, None]
    place = jnp.arange(length, dtype=jnp.int32)
    same = (spot[None, None, :] * SEG) >> shift == place[None, :, None] >> shift
    real = (padding == 1)[:, :, None]
    table = jnp.where(same & real, 0.0, MASKED)
    ones = (spot >= LOG_TOP) & (spot < LOG_TOP + 3)
    table = jnp.where(spot < 8, table, jnp.where(spot == 16, real.astype(F32), jnp.where(ones, 1.0, 0.0)))
    return table.astype(BF16)


X_PAIRS = [(0, 1), (1, 0), (2, 3), (3, 2)]
Y_PAIRS = [(0, 2), (2, 0), (1, 3), (3, 1)]
CROSS = [(0, 3), (3, 0), (1, 2), (2, 1)]


def send(value, pairs, senders=(0, 1, 2, 3)):
    return lax.ppermute(value, "section", [pair for pair in pairs if pair[0] in senders])


def gather_weights(shards):
    section = lax.axis_index("section")
    quarter = lax.dynamic_index_in_dim(shards, section, 0, keepdims=False)
    full = lax.all_gather(quarter, ("dp", "section"), axis=0, tiled=False)
    count = lax.axis_size("dp")
    full = full.reshape((count, lax.axis_size("section")) + quarter.shape)
    return full


def in_quarters(matrix):
    rows, columns = matrix.shape
    return matrix.reshape(rows, 4, columns // 4).transpose(1, 0, 2)


def block_rows(full, kind, by_rows):
    if full.shape[3] % 16 == 0:
        return (full, kind)
    count, quarters, _, rows, width = full.shape
    one = full[:, :, kind]
    if by_rows:
        return (one.reshape(count * rows * quarters // width, quarters, 1, width // quarters, width), 0)
    return (one.transpose(1, 0, 2, 3).reshape(1, quarters, 1, count * rows, width), 0)


def on_device(
    inputs, bucket, padding, cotangent, down_weight, down_bias, up_weight, up_bias, ln_gain, ln_beta, qkv_weight,
    query_bias, value_bias, attn_out_weight, attn_out_bias, ffn_in_weight, ffn_in_bias, ffn_out_weight, ffn_out_bias,
):
    section = lax.axis_index("section")
    early = section < 2
    side = section % 2
    width = inputs.shape[2]
    adapter_width = down_weight.shape[2]
    layers = qkv_weight.shape[0]

    def layer_shards(layer):
        attn = jnp.concatenate([qkv_weight[layer], attn_out_weight[layer]], 1)
        outer = ffn_out_weight[layer]
        return (
            in_quarters(attn)[:, None],
            jnp.stack([in_quarters(ffn_in_weight[layer]), outer.reshape((4, -1) + outer.shape[1:])], 1),
        )

    weights = []
    for layer in range(layers):
        attn, inner = layer_shards(layer)
        if layer == 0:
            attn_full = gather_weights(attn)
            inner_full = gather_weights(inner)
            weights.append([block_rows(attn_full, 0, False), block_rows(inner_full, 0, False), block_rows(inner_full, 1, True)])
        else:
            full = gather_weights(jnp.concatenate([attn, inner], 1))
            weights.append([block_rows(full, 0, False), block_rows(full, 1, False), block_rows(full, 2, True)])

    zero_row = jnp.zeros((1, width), F32)
    own_vecs = jnp.concatenate(
        [zero_row, up_bias, ln_gain, ln_beta, jnp.pad(down_bias, ((0, 0), (0, width - adapter_width))), zero_row, zero_row, zero_row], 0
    )
    own_pack = jnp.concatenate([down_weight[0].T.astype(F32), up_weight[0].astype(F32), own_vecs], 0)
    packs = lax.all_gather(own_pack, "section", axis=0, tiled=False)
    adapters = packs[:, :128].astype(BF16).reshape(layers, 2, 128, width)
    vecs = packs[:, 128:].reshape(layers, 2, 8, width)
    vecs = vecs.at[:, 0, 0].set(attn_out_bias).at[:, 0, 5].set(query_bias).at[:, 0, 6].set(value_bias)
    vecs = vecs.at[:, 1, 0].set(ffn_out_bias).reshape(layers, 16, width)
    in_bias = ffn_in_bias[:, None, :]

    table = key_table(bucket, padding)
    own = section
    shared = 4 + side

    def row_of(array, row):
        return lax.dynamic_index_in_dim(array, row, 0, keepdims=False)

    def forward(row, hidden, layer, weights_used, choice):
        return forward_pair(
            layer, choice, row_of(bucket, row), hidden, row_of(table, row), weights_used, adapters, vecs, in_bias
        )

    def backward(row, grad, saved, layer, weights_used, choice):
        return backward_pair(
            layer, choice, row_of(bucket, row), grad, row_of(table, row), saved, weights_used, adapters, vecs
        )

    zero = jnp.int32(0)
    one = jnp.int32(1)
    late = 1 - early.astype(jnp.int32)
    first_row = jnp.where(early, shared, own)
    third_row = jnp.where(early, own, shared)

    f0 = forward(first_row, row_of(inputs, first_row), zero, weights[:1], zero)
    x0 = send(jnp.where(side == 0, f0[1], f0[0]), X_PAIRS, (0, 1))
    y0 = send(jnp.where(early | (side == 1), f0[1], f0[0]), Y_PAIRS)
    z0 = send(jnp.where(side == 0, f0[1], f0[0]), CROSS, (2, 3))
    hidden = jnp.where(early, row_of(inputs, own), f0[1])
    f1 = forward(own, hidden, late, weights, late)
    x1 = send(jnp.where(side == 0, f1[1], f1[0]), X_PAIRS)
    hidden = jnp.where(early, f1[1], y0)
    f2 = forward(third_row, hidden, one, weights[1:], zero)
    x2 = send(jnp.where(side == 0, f2[1], f2[0]), X_PAIRS, (2, 3))
    y2 = send(jnp.where(side == 1, f2[1], f2[0]), Y_PAIRS, (0, 1))
    z2 = send(jnp.where(side == 0, f2[1], f2[0]), CROSS, (0, 1))

    b3 = backward(third_row, row_of(cotangent, third_row), f2[2:11], one, weights[1:], zero)
    x3 = send(jnp.where(side == 0, b3[0], b3[1]), X_PAIRS, (2, 3))
    y3 = send(jnp.where(early & (side == 1), b3[0], b3[1]), Y_PAIRS)
    z3 = send(jnp.where(side == 0, b3[0], b3[1]), CROSS, (0, 1))
    grad = jnp.where(early, b3[1], row_of(cotangent, own))
    b4 = backward(own, grad, f1[2:11], late, weights, late)
    x4 = send(jnp.where(side == 0, b4[0], b4[1]), X_PAIRS)
    grad = jnp.where(early, y3, b4[1])
    b5 = backward(first_row, grad, f0[2:11], zero, weights[:1], zero)
    x5 = send(jnp.where(side == 0, b5[0], b5[1]), X_PAIRS, (0, 1))
    y5 = send(jnp.where(side == 1, b5[0], b5[1]), Y_PAIRS, (2, 3))
    z5 = send(jnp.where(side == 0, b5[0], b5[1]), CROSS, (2, 3))

    def assemble(parts):
        result = jnp.zeros(inputs.shape, BF16)
        for row, part in parts:
            result = lax.dynamic_update_index_in_dim(result, part, row, 0)
        return result

    other = section + 1 - 2 * side
    across = jnp.where(early, section + 2, section - 2)
    corner = 3 - section
    other_shared = 4 + 1 - side
    outputs = assemble(
        [
            (own, jnp.where(side == 0, f1[0], f1[1])),
            (other, x1),
            (across, jnp.where(early, y0, y2)),
            (corner, jnp.where(early, z0, z2)),
            (shared, jnp.where(early, jnp.where(side == 0, f0[0], f0[1]), jnp.where(side == 0, f2[0], f2[1]))),
            (other_shared, jnp.where(early, x0, x2)),
        ]
    )
    input_grads = assemble(
        [
            (own, jnp.where(side == 0, b4[1], b4[0])),
            (other, x4),
            (across, jnp.where(early, y5, y3)),
            (corner, jnp.where(early, z5, z3)),
            (shared, jnp.where(early, jnp.where(side == 0, b5[1], b5[0]), jnp.where(side == 0, b3[1], b3[0]))),
            (other_shared, jnp.where(early, x5, x3)),
        ]
    )

    def with_sums(grads, sums):
        squares = jnp.sum(sums[:4].reshape(2, 2, width), -1, keepdims=True)
        return grads.at[:, 132:134].set(jnp.broadcast_to(squares, (2, 2, width)))

    g3, g4, g5 = with_sums(b3[2], f2[11]), with_sums(b4[2], f1[11]), with_sums(b5[2], f0[11])
    low_layer = g5 + jnp.where(early, g4, 0.0)
    high_layer = g3 + jnp.where(early, 0.0, g4)
    mine = lax.psum_scatter(jnp.concatenate([low_layer, high_layer], 0), "section", scatter_dimension=0, tiled=False)
    total = lax.psum(mine, "dp")
    ratios = jnp.sqrt(total[132, 0] / total[133, 0])[None]
    return (
        outputs[None],
        input_grads[None],
        total[64:128].T[None],
        total[131, :adapter_width][None],
        total[0:64][None],
        total[128][None],
        total[129][None],
        total[130][None],
        ratios,
    )


def solution(mesh):
    in_specs = (
        P("dp", None, None),
        P("dp"),
        P("dp", None),
        P("dp", None, None),
        P("section", None, None),
        P("section", None),
        P("section", None, None),
        P("section", None),
        P("section", None),
        P("section", None),
        P(None, "dp", None),
        P(),
        P(),
        P(None, "dp", None),
        P(),
        P(None, "dp", None),
        P(),
        P(None, "dp", None),
        P(),
    )
    out_specs = (
        P("section", "dp", None, None),
        P("section", "dp", None, None),
        P("section", None, None),
        P("section", None),
        P("section", None, None),
        P("section", None),
        P("section", None),
        P("section", None),
        P("section"),
    )
    return jax.shard_map(
        on_device, mesh=mesh, in_specs=in_specs, out_specs=out_specs, check_vma=False
    )
```

time: 1720 us -> 681 us (0.40)
  local copies, waits for them, and re-layouts: 430 us -> 41.8 us
  matrix products: 372 us -> 0 us
  other arithmetic: 411 us -> 44.7 us
  Pallas kernels: 0 us -> 207 us
  loops' own time: 43.8 us -> 0 us
  starting transfers between devices: 69.9 us -> 31.1 us
  blocking collectives: 26.1 us -> 0 us
    dot_general x102 -> x0, matrix products: 372 us -> none  [the longest x24 81.2 us: product(): return jnp.dot(left, right, preferred_element_type=jnp.float32)]
    pallas_call x0 -> x6, Pallas kernels: none -> 207 us  [call_with_weights(): pl.pallas_call(body, grid_spec=pltpu.PrefetchScalarGridSpec(num_scalar_pr...]
    dynamic_slice x98 -> x3, local copies, waits for them, and re-layouts: 208 us -> 2.16 us  [the longest x2 1.57 us: gather_weights(): quarter = lax.dynamic_index_in_dim(shards, section, 0, keepdims=False)]
    ppermute x18 -> x14, waiting for transfers between devices: 207 us -> 57.2 us  [send(): lax.ppermute(value, 'section', [pair for pair in pairs if pair[0] in send...]
    dynamic_update_slice x54 -> x10, other arithmetic: 145 us -> 13.5 us  [assemble(): result = lax.dynamic_update_index_in_dim(result, part, row, 0)]
    all_gather x2 -> x4, waiting for transfers between devices: 97.5 us -> 224 us  [the longest x3 215 us: gather_weights(): full = lax.all_gather(quarter, ('dp', 'section'), axis=0, tiled=False)]
    reduce_sum x48 -> x3, other arithmetic: 90.8 us -> 0.35 us  [with_sums(): squares = jnp.sum(sums[:4].reshape(2, 2, width), -1, keepdims=True)]
    another operation x49 -> x9, local copies, waits for them, and re-layouts: 69.6 us -> 3.29 us
  transfers between devices with their start and end apart: 21 -> 20, of which waited for: 12 -> 7; matrix products, arithmetic and copies ran while one was open for 26% -> 11% of each run, Pallas kernels for 0% -> 31%
where the time goes in v1:
time: 681 us; the launch traced here: 678 us
  waiting for transfers between devices  336 us (49%)
  Pallas kernels  207 us (30%)
  other arithmetic  44.7 us (7%)
  local copies, waits for them, and re-layouts  41.8 us (6%)
  starting transfers between devices  31.1 us (5%)
  between operations  17.5 us (3%)
    all_gather x3, waiting for transfers between devices, gather_weights(): full = lax.all_gather(quarter, ('dp', 'section'), axis=0, tiled=False)  215 us
    pallas_call x6, Pallas kernels, call_with_weights(): pl.pallas_call(body, grid_spec=pltpu.PrefetchScalarGridSpec(num_scalar_pr...  207 us
    ppermute x14, waiting for transfers between devices, send(): lax.ppermute(value, 'section', [pair for pair in pairs if pair[0] in send...  57.2 us
    psum x1, waiting for transfers between devices, on_device(): total = lax.psum(mine, 'dp')  54.2 us
    ppermute x14, starting transfers between devices, send(): lax.ppermute(value, 'section', [pair for pair in pairs if pair[0] in send...  30.8 us
  transfers between devices with their start and end apart: 20, of which 7 were waited for; matrix products, arithmetic and copies ran while one was open for 11% of the time, Pallas kernels for 31%

profile of v1, /device:TPU:0, one launch (start us, length us, event | category | flops | bytes accessed | tf_op | source)
XLA Modules:
  0.0 677.7 jit_solution(13680580975183468025)
XLA Ops:
  9.8 2.7 concatenate.40
  33.9 2.1 dynamic-slice_bitcast_fusion.1.refs_1_
  36.0 2.1 dynamic-slice_bitcast_fusion.refs_1_
  38.0 9.2 %all-gather.11.cloned.1.call-done = f32[544,768]{1,0:T(8,128)} async-done(((f32[136,768]{1,0:T(8,128)}), f32[544,768]{1,0:T(8,128)}) %all-gather.11.cloned.1.call-update) | async-done | bytes 1671184 | tf_op jit(solution)/shard_map/all_gather | solution.py:515
  48.1 2.4 slice.295
  57.4 56.9 %all-gather.13.cloned.1.call-done = bf16[3072,1,768]{2,0,1:T(8,128)(2,1)} async-done(((bf16[96,1,768]{2,0,1:T(8,128)(2,1)}), bf16[3072,1,768]{2,0,1:T(8,128)(2,1)}) %all-gather.13.cloned.1.call-update) | async-done | bytes 4718608 | tf_op jit(solution)/shard_map/all_gather | solution.py:459
  114.3 83.8 %all-gather.7.cloned.1.call-done = bf16[32,2,96,768]{3,2,1,0:T(8,128)(2,1)} async-done(((bf16[1,2,96,768]{3,2,1,0:T(8,128)(2,1)}), bf16[32,2,96,768]{3,2,1,0:T(8,128)(2,1)}) %all-gather.7.cloned.1.call-update) | async-done | bytes 9437200 | tf_op jit(solution)/shard_map/all_gather | solution.py:459
  198.1 43.9 %forward_pair.3 = (bf16[512,768]{1,0:T(8,128)(2,1)}, bf16[512,768]{1,0:T(8,128)(2,1)}, bf16[512,2304]{1,0:T(8,128)(2,1)}, bf16[512,768]{1,0:T(8,128)(2,1)}, bf16...) custom-call(s32[3]{0:T(128)} %pad_add_fusion.1.refs_0_, ...), custom_call_target="tpu_custom_call" | custom-call | flops 12000000000 | bytes 24000000 | tf_op jit(solution)/shard_map/forward_pair/pallas_call | solution.py:251
  242.0 2.9 broadcast_select_fusion.10
  246.2 3.4 collective-permute-start.5
  249.6 2.6 collective-permute-start.1
  252.5 74.3 %all-gather.9.cloned.1.call-done = bf16[32,3,96,768]{3,2,1,0:T(8,128)(2,1)} async-done(((bf16[1,3,96,768]{3,2,1,0:T(8,128)(2,1)}), bf16[32,3,96,768]{3,2,1,0:T(8,128)(2,1)}) %all-gather.9.cloned.1.call-update) | async-done | bytes 14155792 | tf_op jit(solution)/shard_map/all_gather | solution.py:459
  326.7 32.0 %forward_pair.4 = (bf16[512,768]{1,0:T(8,128)(2,1)}, bf16[512,768]{1,0:T(8,128)(2,1)}, bf16[512,2304]{1,0:T(8,128)(2,1)}, bf16[512,768]{1,0:T(8,128)(2,1)}, bf16...) custom-call(s32[3]{0:T(128)} %pad_add_fusion.6.refs_0_, ...), custom_call_target="tpu_custom_call" | custom-call | flops 12000000000 | bytes 24000000 | tf_op jit(solution)/shard_map/forward_pair/pallas_call | solution.py:251
  358.8 2.4 broadcast_select_fusion.5
  361.2 31.8 %forward_pair.5 = (bf16[512,768]{1,0:T(8,128)(2,1)}, bf16[512,768]{1,0:T(8,128)(2,1)}, bf16[512,2304]{1,0:T(8,128)(2,1)}, bf16[512,768]{1,0:T(8,128)(2,1)}, bf16...) custom-call(s32[3]{0:T(128)} %pad_add_fusion.refs_0_, ...), custom_call_target="tpu_custom_call" | custom-call | flops 12000000000 | bytes 24000000 | tf_op jit(solution)/shard_map/forward_pair/pallas_call | solution.py:251
  393.0 32.8 %backward_pair.3 = (bf16[512,768]{1,0:T(8,128)(2,1)}, bf16[512,768]{1,0:T(8,128)(2,1)}, f32[2,136,768]{2,1,0:T(8,128)}) custom-call(s32[3]{0:T(128)} %pad_add_fusion.refs_0_, bf16[512,768]{1,0:T(8,128)(2,1)} %dynamic-slice_bitcast_fusion.refs_1_, bf16[512,128]{1,0:T(8,128)(2,1)} %get-tuple-element.207.refs_2_, bf16[512,2304]{1,0:T(8,128)(2,1)} %get-tuple-element.144.refs_3_, ...), custom_call_target="tpu_custom_call" | custom-call | flops 16000000000 | bytes 24000000 | tf_op jit(solution)/shard_map/backward_pair/pallas_call | solution.py:251
  425.9 3.3 broadcast_select_fusion.6
  430.5 5.2 collective-permute-start.2
  437.4 33.2 %backward_pair.4 = (bf16[512,768]{1,0:T(8,128)(2,1)}, bf16[512,768]{1,0:T(8,128)(2,1)}, f32[2,136,768]{2,1,0:T(8,128)}) custom-call(s32[3]{0:T(128)} %pad_add_fusion.6.refs_0_, bf16[512,768]{1,0:T(8,128)(2,1)} %get-tuple-element.203.refs_1_, bf16[512,128]{1,0:T(8,128)(2,1)} %get-tuple-element.208.refs_2_, bf16[512,2304]{1,0:T(8,128)(2,1)} %get-tuple-element.154.refs_3_, ...), custom_call_target="tpu_custom_call" | custom-call | flops 16000000000 | bytes 24000000 | tf_op jit(solution)/shard_map/backward_pair/pallas_call | solution.py:251
  472.4 3.9 collective-permute-start.4
  476.3 2.7 broadcast_select_fusion.4
  479.0 33.1 %backward_pair.5 = (bf16[512,768]{1,0:T(8,128)(2,1)}, bf16[512,768]{1,0:T(8,128)(2,1)}, f32[2,136,768]{2,1,0:T(8,128)}) custom-call(s32[3]{0:T(128)} %pad_add_fusion.1.refs_0_, bf16[512,768]{1,0:T(8,128)(2,1)} %get-tuple-element.204.refs_1_, bf16[512,128]{1,0:T(8,128)(2,1)} %get-tuple-element.209.refs_2_, bf16[512,2304]{1,0:T(8,128)(2,1)} %get-tuple-element.166.refs_3_, ...), custom_call_target="tpu_custom_call" | custom-call | flops 16000000000 | bytes 24000000 | tf_op jit(solution)/shard_map/backward_pair/pallas_call | solution.py:251
  515.6 2.5 broadcast_in_dim.124.clone.1
  519.2 2.5 broadcast_in_dim.124.clone
  523.6 2.1 bitcast_dynamic-update-slice_fusion.10
  526.7 4.3 collective-permute-start.11
  535.3 2.2 bitcast_dynamic-update-slice_fusion.8
  541.0 2.2 bitcast_dynamic-update-slice_fusion.6
  543.2 29.7 %collective-permute-done.7 = bf16[512,768]{1,0:T(8,128)(2,1)S(1)} collective-permute-done((bf16[512,768]{1,0:T(8,128)(2,1)S(1)}, bf16[512,768]{1,0:T(8,128)(2,1)S(1)}, u32[]{:S(2)}, u32[]{:S(2)}) %collective-permute-start.7) | collective-permute-done | bytes 786464 | tf_op jit(solution)/shard_map/ppermute | solution.py:453
  573.0 2.2 collective-permute-start.12
  577.2 27.5 %collective-permute-done.10 = bf16[512,768]{1,0:T(8,128)(2,1)S(1)} collective-permute-done((bf16[512,768]{1,0:T(8,128)(2,1)}, bf16[512,768]{1,0:T(8,128)(2,1)S(1)}, u32[]{:S(2)}, u32[]{:S(2)}) %collective-permute-start.10) | collective-permute-done | bytes 786464 | tf_op jit(solution)/shard_map/ppermute | solution.py:453
  608.2 54.2 %all-reduce.4.cloned.1.call-done = f32[136,768]{1,0:T(8,128)} async-done(((f32[136,768]{1,0:T(8,128)}), f32[136,768]{1,0:T(8,128)}) %all-reduce.4.cloned.1.call-update) | async-done | bytes 417808 | tf_op jit(solution)/shard_map/psum | solution.py:610
  (166 shorter events, 63.9 us)
Async XLA Ops:
  7.2 40.0 %all-gather.11.cloned.1.call-start = ((), (), s32[]{:S(2)}) async-start(), calls=%async_computation.4 | async-start | bytes 2088960 | tf_op jit(solution)/shard_map/all_gather | solution.py:515
  12.6 101.7 %all-gather.13.cloned.1.call-start = ((), (), s32[]{:S(2)}) async-start(), calls=%async_computation.5 | async-start | bytes 4866048 | tf_op jit(solution)/shard_map/all_gather | solution.py:459
  16.4 181.6 %all-gather.7.cloned.1.call-start = ((), (), s32[]{:S(2)}) async-start(), calls=%async_computation.1 | async-start | bytes 9732096 | tf_op jit(solution)/shard_map/all_gather | solution.py:459
  19.6 11.8 %copy-start.19 = (s32[6,512]{1,0:T(8,128)S(1)}, s32[6,512]{1,0:T(8,128)}, u32[]{:S(2)}) copy-start(s32[6,512]{1,0:T(8,128)} %param.35) | copy-start | bytes 36868
  20.4 306.3 %all-gather.9.cloned.1.call-start = ((), (), s32[]{:S(2)}) async-start(), calls=%async_computation.2 | async-start | bytes 14598144 | tf_op jit(solution)/shard_map/all_gather | solution.py:459
  23.3 27.2 %copy-start.25 = (f32[2,768]{1,0:T(2,128)S(1)}, f32[2,768]{1,0:T(2,128)}, u32[]{:S(2)}) copy-start(f32[2,768]{1,0:T(2,128)} %param.44) | copy-start | bytes 18436
  23.3 30.7 %copy-start.26 = (f32[2,768]{1,0:T(2,128)S(1)}, f32[2,768]{1,0:T(2,128)}, u32[]{:S(2)}) copy-start(f32[2,768]{1,0:T(2,128)} %param.45) | copy-start | bytes 18436
  24.2 582.9 %reduce-scatter.4.cloned.1.call-start = ((), (), s32[]{:S(2)}) async-start(), calls=%async_computation.6 | async-start | bytes 2088960
  57.4 140.7 %copy-start.17 = (f32[2,2,8,768]{3,2,1,0:T(8,128)}, f32[2,2,8,768]{3,2,1,0:T(8,128)S(1)}, u32[]{:S(2)}) copy-start(f32[2,2,8,768]{3,2,1,0:T(8,128)S(1)} %scatter.29) | copy-start | bytes 294916
  244.9 287.2 %collective-permute-start.3 = (bf16[512,768]{1,0:T(8,128)(2,1)}, bf16[512,768]{1,0:T(8,128)(2,1)}, u32[]{:S(2)}, u32[]{:S(2)}) collective-permute-start(bf16[512,768]{1,0:T(8,128)(2,1)} %get-tuple-element.193), channel_id=1, source_target_pairs={{24,0},{16,8},{25,1},{17,9},{26,2},{18,10},{27,3},{19,11},{28,4},{... | collective-permute-start | bytes 2359304 | tf_op jit(solution)/shard_map/ppermute | solution.py:453
  246.2 292.6 %collective-permute-start.5 = (bf16[512,768]{1,0:T(8,128)(2,1)}, bf16[512,768]{1,0:T(8,128)(2,1)}, u32[]{:S(2)}, u32[]{:S(2)}) collective-permute-start(bf16[512,768]{1,0:T(8,128)(2,1)} %get-tuple-element.193), channel_id=1, source_target_pairs={{0,8},{8,0},{1,9},{9,1},{2,10},{10,2},{3,11},{11,3},{4,12},{12,4},... | collective-permute-start | bytes 2359304 | tf_op jit(solution)/shard_map/ppermute | solution.py:453
  249.6 109.1 %collective-permute-start.1 = (bf16[512,768]{1,0:T(8,128)(2,1)S(1)}, bf16[512,768]{1,0:T(8,128)(2,1)S(1)}, u32[]{:S(2)}, u32[]{:S(2)}) collective-permute-start(bf16[512,768]{1,0:T(8,128)(2,1)S(1)} %get-tuple-element.194), channel_id=1, source_target_pairs={{0,16},{16,0},{8,24},{24,8},{1,17},{17,1},{9,25},{25,9},{2,18},{18... | collective-permute-start | bytes 2359304 | tf_op jit(solution)/shard_map/ppermute | solution.py:453
  429.2 43.2 %collective-permute-start.8 = (bf16[512,768]{1,0:T(8,128)(2,1)}, bf16[512,768]{1,0:T(8,128)(2,1)S(1)}, u32[]{:S(2)}, u32[]{:S(2)}) collective-permute-start(bf16[512,768]{1,0:T(8,128)(2,1)} %get-tuple-element.188), channel_id=1, source_target_pairs={{0,16},{16,0},{8,24},{24,8},{1,17},{17,1},{9,25},{25,9},{2,18},{18... | collective-permute-start | bytes 2359304 | tf_op jit(solution)/shard_map/ppermute | solution.py:453
  430.5 96.2 %collective-permute-start.2 = (bf16[512,768]{1,0:T(8,128)(2,1)}, bf16[512,768]{1,0:T(8,128)(2,1)}, u32[]{:S(2)}, u32[]{:S(2)}) collective-permute-start(bf16[512,768]{1,0:T(8,128)(2,1)} %get-tuple-element.192), channel_id=1, source_target_pairs={{0,16},{8,24},{1,17},{9,25},{2,18},{10,26},{3,19},{11,27},{4,20},{... | collective-permute-start | bytes 2359304 | tf_op jit(solution)/shard_map/ppermute | solution.py:453
  435.7 87.0 %collective-permute-start = (bf16[512,768]{1,0:T(8,128)(2,1)}, bf16[512,768]{1,0:T(8,128)(2,1)}, u32[]{:S(2)}, u32[]{:S(2)}) collective-permute-start(bf16[512,768]{1,0:T(8,128)(2,1)} %get-tuple-element.211), channel_id=1, source_target_pairs={{0,8},{8,0},{16,24},{24,16},{1,9},{9,1},{17,25},{25,17},{2,10},{10... | collective-permute-start | bytes 2359304 | tf_op jit(solution)/shard_map/ppermute | solution.py:453
  437.4 33.2 %copy-start.21 = (f32[8,768]{1,0:T(8,128)S(1)}, f32[8,768]{1,0:T(8,128)}, u32[]{:S(2)}) copy-start(f32[8,768]{1,0:T(8,128)} %get-tuple-element.182) | copy-start | bytes 73732
  437.4 33.4 %copy-start.20 = (f32[8,768]{1,0:T(8,128)S(1)}, f32[8,768]{1,0:T(8,128)}, u32[]{:S(2)}) copy-start(f32[8,768]{1,0:T(8,128)} %get-tuple-element.180) | copy-start | bytes 73732
  472.4 61.0 %collective-permute-start.4 = (bf16[512,768]{1,0:T(8,128)(2,1)}, bf16[512,768]{1,0:T(8,128)(2,1)}, u32[]{:S(2)}, u32[]{:S(2)}) collective-permute-start(bf16[512,768]{1,0:T(8,128)(2,1)} %get-tuple-element.191), channel_id=1, source_target_pairs={{0,24},{8,16},{1,25},{9,17},{2,26},{10,18},{3,27},{11,19},{4,28},{... | collective-permute-start | bytes 2359304 | tf_op jit(solution)/shard_map/ppermute | solution.py:453
  479.0 33.8 %copy-start.13 = (f32[2,136,768]{2,1,0:T(8,128)S(1)}, f32[2,136,768]{2,1,0:T(8,128)}, u32[]{:S(2)}) copy-start(f32[2,136,768]{2,1,0:T(8,128)} %constant_dynamic-update-slice_fusion) | copy-start | bytes 2506756
  479.0 33.8 %copy-start.14 = (f32[2,136,768]{2,1,0:T(8,128)S(1)}, f32[2,136,768]{2,1,0:T(8,128)}, u32[]{:S(2)}) copy-start(f32[2,136,768]{2,1,0:T(8,128)} %constant_dynamic-update-slice_fusion.1) | copy-start | bytes 2506756
  515.5 146.9 %all-reduce.4.cloned.1.call-start = ((), (), s32[]{:S(2)}) async-start(), calls=%async_computation.3 | async-start | bytes 835584 | tf_op jit(solution)/shard_map/psum | solution.py:610
  522.7 14.8 %copy-start.8 = (bf16[512,768]{1,0:T(8,128)(2,1)S(1)}, bf16[512,768]{1,0:T(8,128)(2,1)}, u32[]{:S(2)}) copy-start(bf16[512,768]{1,0:T(8,128)(2,1)} %get-tuple-element.141) | copy-start | bytes 2359300
  522.7 14.8 %copy-start.9 = (bf16[512,768]{1,0:T(8,128)(2,1)S(1)}, bf16[512,768]{1,0:T(8,128)(2,1)}, u32[]{:S(2)}) copy-start(bf16[512,768]{1,0:T(8,128)(2,1)} %get-tuple-element.138) | copy-start | bytes 2359300
  522.8 16.9 %collective-permute-start.6 = (bf16[512,768]{1,0:T(8,128)(2,1)S(1)}, bf16[512,768]{1,0:T(8,128)(2,1)S(1)}, u32[]{:S(2)}, u32[]{:S(2)}) collective-permute-start(bf16[512,768]{1,0:T(8,128)(2,1)S(1)} %copy-done.15), channel_id=1, source_target_pairs={{16,24},{24,16},{17,25},{25,17},{18,26},{26,18},{19,27},{27,19},{2... | collective-permute-start | bytes 2359304 | tf_op jit(solution)/shard_map/ppermute | solution.py:453
  526.7 50.5 %collective-permute-start.11 = (bf16[512,768]{1,0:T(8,128)(2,1)}, bf16[512,768]{1,0:T(8,128)(2,1)S(1)}, u32[]{:S(2)}, u32[]{:S(2)}) collective-permute-start(bf16[512,768]{1,0:T(8,128)(2,1)} %get-tuple-element.187), channel_id=1, source_target_pairs={{0,24},{8,16},{1,25},{9,17},{2,26},{10,18},{3,27},{11,19},{4,28},{... | collective-permute-start | bytes 2359304 | tf_op jit(solution)/shard_map/ppermute | solution.py:453
  532.1 44.0 %collective-permute-start.9 = (bf16[512,768]{1,0:T(8,128)(2,1)S(1)}, bf16[512,768]{1,0:T(8,128)(2,1)S(1)}, u32[]{:S(2)}, u32[]{:S(2)}) collective-permute-start(bf16[512,768]{1,0:T(8,128)(2,1)S(1)} %get-tuple-element.190), channel_id=1, source_target_pairs={{16,0},{24,8},{17,1},{25,9},{18,2},{26,10},{19,3},{27,11},{20,4},{... | collective-permute-start | bytes 2359304 | tf_op jit(solution)/shard_map/ppermute | solution.py:453
  533.4 39.6 %collective-permute-start.7 = (bf16[512,768]{1,0:T(8,128)(2,1)S(1)}, bf16[512,768]{1,0:T(8,128)(2,1)S(1)}, u32[]{:S(2)}, u32[]{:S(2)}) collective-permute-start(bf16[512,768]{1,0:T(8,128)(2,1)S(1)} %copy-done.16), channel_id=1, source_target_pairs={{0,8},{8,0},{16,24},{24,16},{1,9},{9,1},{17,25},{25,17},{2,10},{10... | collective-permute-start | bytes 2359304 | tf_op jit(solution)/shard_map/ppermute | solution.py:453
  538.8 66.9 %copy-start.10 = (bf16[512,768]{1,0:T(8,128)(2,1)S(1)}, bf16[512,768]{1,0:T(8,128)(2,1)}, u32[]{:S(2)}) copy-start(bf16[512,768]{1,0:T(8,128)(2,1)} %get-tuple-element.165) | copy-start | bytes 2359300
  538.8 66.9 %copy-start.11 = (bf16[512,768]{1,0:T(8,128)(2,1)S(1)}, bf16[512,768]{1,0:T(8,128)(2,1)}, u32[]{:S(2)}) copy-start(bf16[512,768]{1,0:T(8,128)(2,1)} %get-tuple-element.153) | copy-start | bytes 2359300
  538.8 68.3 %collective-permute-start.13 = (bf16[512,768]{1,0:T(8,128)(2,1)}, bf16[512,768]{1,0:T(8,128)(2,1)S(1)}, u32[]{:S(2)}, u32[]{:S(2)}) collective-permute-start(bf16[512,768]{1,0:T(8,128)(2,1)} %get-tuple-element.187), channel_id=1, source_target_pairs={{16,24},{24,16},{17,25},{25,17},{18,26},{26,18},{19,27},{27,19},{2... | collective-permute-start | bytes 2359304 | tf_op jit(solution)/shard_map/ppermute | solution.py:453
  539.7 65.0 %collective-permute-start.10 = (bf16[512,768]{1,0:T(8,128)(2,1)}, bf16[512,768]{1,0:T(8,128)(2,1)S(1)}, u32[]{:S(2)}, u32[]{:S(2)}) collective-permute-start(bf16[512,768]{1,0:T(8,128)(2,1)} %get-tuple-element.189), channel_id=1, source_target_pairs={{24,0},{16,8},{25,1},{17,9},{26,2},{18,10},{27,3},{19,11},{28,4},{... | collective-permute-start | bytes 2359304 | tf_op jit(solution)/shard_map/ppermute | solution.py:453
  573.0 34.2 %collective-permute-start.12 = (bf16[512,768]{1,0:T(8,128)(2,1)}, bf16[512,768]{1,0:T(8,128)(2,1)S(1)}, u32[]{:S(2)}, u32[]{:S(2)}) collective-permute-start(bf16[512,768]{1,0:T(8,128)(2,1)} %get-tuple-element.189), channel_id=1, source_target_pairs={{0,8},{8,0},{1,9},{9,1},{2,10},{10,2},{3,11},{11,3},{4,12},{12,4},... | collective-permute-start | bytes 2359304 | tf_op jit(solution)/shard_map/ppermute | solution.py:453
  (17 other events, 98.3 us)
Sparse Core Ops, SparseCore 0:
  12.7 34.4 all-gather.10
  50.7 63.5 all-gather.12
  117.2 80.8 all-gather.6
  200.8 125.8 all-gather.8
  515.6 50.6 reduce-scatter.3
  607.2 55.1 all-reduce.3

commit v2 on v1

--- a/solution.py
+++ b/solution.py
@@ -444,6 +444,227 @@
     return table.astype(BF16)
 
 
+MESH = pl.DeviceIdType.MESH
+
+
+def place_of(index):
+    return index // 2, index % 2
+
+
+class Gather:
+    def __init__(self, full, sems):
+        self.full = full
+        self.sems = sems
+        self.section = lax.axis_index("section")
+        self.dp = lax.axis_index("dp")
+        self.count = lax.axis_size("dp") // 2
+        self.z, self.core = place_of(self.dp)
+        self.x_side = self.section + 1 - 2 * (self.section % 2)
+        self.y_side = lax.rem(self.section + 2, 4)
+        self.corner = 3 - self.section
+        self.sibling = self.dp + 1 - 2 * self.core
+
+    def along(self, step):
+        return lax.rem(self.z + step, self.count) * 2 + self.core
+
+    def source(self, step):
+        return lax.rem(self.z + self.count - step, self.count) * 2 + self.core
+
+    def peers(self):
+        steps = [(self.section, self.along(d)) for d in range(1, self.count)]
+        near = [(other, self.dp) for other in (self.x_side, self.y_side, self.corner)]
+        return steps + near + [(self.section, self.sibling)]
+
+    def barrier(self):
+        entry = pltpu.get_barrier_semaphore()
+        peers = self.peers()
+        for peer in peers:
+            pl.semaphore_signal(entry, inc=1, device_id=peer, device_id_type=MESH)
+        pl.semaphore_wait(entry, len(peers))
+
+    def block(self, layer, group, shard, quarter, rows=None):
+        kinds = pl.ds(0, 1) if group == 0 else pl.ds(1, 2)
+        ref = self.full[layer].at[shard, quarter, kinds]
+        return ref if rows is None else ref.at[:, rows]
+
+    def copy(self, ref, name, spot, device):
+        return pltpu.make_async_remote_copy(
+            src_ref=ref, dst_ref=ref, send_sem=self.sems[name].at[(0,) + spot], recv_sem=self.sems[name].at[(1,) + spot],
+            device_id=device, device_id_type=MESH,
+        )
+
+    def z_copy(self, layer, group, step):
+        ref = self.block(layer, group, self.dp, self.section)
+        return self.copy(ref, "z", (layer, group, step - 1), (self.section, self.along(step)))
+
+    def side_copy(self, layer, group, step, way):
+        ref = self.block(layer, group, self.source(step), self.section)
+        device = (self.x_side if way == 0 else self.y_side, self.dp)
+        return self.copy(ref, "side", (layer, group, step - 1, way), device)
+
+    def corner_copy(self, layer, group, step, way):
+        half = self.full[layer].shape[3] // 2
+        quarter, target = (self.x_side, self.y_side) if way == 0 else (self.y_side, self.x_side)
+        ref = self.block(layer, group, self.source(step), quarter, pl.ds(way * half, half))
+        return self.copy(ref, "corner", (layer, group, step - 1, way), (target, self.dp))
+
+    def core_copy(self, layer, group, step, which):
+        quarter = (self.section, self.x_side, self.y_side, self.corner)[which]
+        ref = self.block(layer, group, self.source(step), quarter)
+        return self.copy(ref, "core", (layer, group, step, which), (self.section, self.sibling))
+
+    def steps(self):
+        return range(1, self.count)
+
+    def start(self, layer, group):
+        for step in self.steps():
+            self.z_copy(layer, group, step).start()
+        for which in range(4):
+            self.core_copy(layer, group, 0, which).start()
+
+    def spread(self, layer, group):
+        for step in self.steps():
+            self.z_copy(layer, group, step).wait_recv()
+            for way in range(2):
+                self.side_copy(layer, group, step, way).start()
+            self.core_copy(layer, group, step, 0).start()
+
+    def relay(self, layer, group):
+        for step in self.steps():
+            for way in range(2):
+                self.side_copy(layer, group, step, way).wait_recv()
+                self.corner_copy(layer, group, step, way).start()
+                self.core_copy(layer, group, step, 1 + way).start()
+
+    def close(self, layer, group):
+        for step in self.steps():
+            for way in range(2):
+                self.corner_copy(layer, group, step, way).wait_recv()
+            self.core_copy(layer, group, step, 3).start()
+
+    def arrive(self, layer, group):
+        for step in range(self.count):
+            for which in range(4):
+                self.core_copy(layer, group, step, which).wait_recv()
+
+    def drain(self, layer, group):
+        for step in self.steps():
+            self.z_copy(layer, group, step).wait_send()
+            for way in range(2):
+                self.side_copy(layer, group, step, way).wait_send()
+                self.corner_copy(layer, group, step, way).wait_send()
+        for step in range(self.count):
+            for which in range(4):
+                self.core_copy(layer, group, step, which).wait_send()
+
+    @staticmethod
+    def semaphores(count):
+        return {
+            "z": pltpu.SemaphoreType.DMA((2, 2, 2, count - 1)),
+            "side": pltpu.SemaphoreType.DMA((2, 2, 2, count - 1, 2)),
+            "corner": pltpu.SemaphoreType.DMA((2, 2, 2, count - 1, 2)),
+            "core": pltpu.SemaphoreType.DMA((2, 2, 2, count, 4)),
+        }
+
+
+def own_blocks(full, layer, shard, qkv_w, attn_w, in_w, out_w, sems):
+    width = full.shape[-1]
+    rows = full.shape[3]
+    made = []
+    for quarter in range(4):
+        cols = pl.ds(quarter * width, width)
+        first = qkv_w.at[layer, :, cols] if quarter < 3 else attn_w.at[layer]
+        made.append(pltpu.make_async_copy(first, full.at[shard, quarter, 0], sems.at[layer, 3 * quarter]))
+        made.append(pltpu.make_async_copy(in_w.at[layer, :, cols], full.at[shard, quarter, 1], sems.at[layer, 3 * quarter + 1]))
+        made.append(
+            pltpu.make_async_copy(
+                out_w.at[layer, pl.ds(quarter * rows, rows)], full.at[shard, quarter, 2], sems.at[layer, 3 * quarter + 2]
+            )
+        )
+    return made
+
+
+def small_copies(gather, ref, sems, base):
+    made = []
+    for i, target in enumerate((gather.x_side, gather.y_side, gather.corner)):
+        made.append(
+            pltpu.make_async_remote_copy(
+                src_ref=ref.at[gather.section], dst_ref=ref.at[gather.section], send_sem=sems.at[0, base + i],
+                recv_sem=sems.at[1, base + i], device_id=(target, gather.dp), device_id_type=MESH,
+            )
+        )
+    return made
+
+
+def gather_kernel(
+    qkv_w, attn_w, in_w, out_w, own_adapter, own_vec, full0, full1, adapters, vecs,
+    z_sem, side_sem, corner_sem, core_sem, small_sem, local_sem,
+):
+    gather = Gather([full0, full1], {"z": z_sem, "side": side_sem, "corner": corner_sem, "core": core_sem})
+    local = [own_blocks(full, layer, gather.dp, qkv_w, attn_w, in_w, out_w, local_sem) for layer, full in enumerate((full0, full1))]
+    tiny = [
+        pltpu.make_async_copy(own_adapter, adapters.at[gather.section], local_sem.at[2, 0]),
+        pltpu.make_async_copy(own_vec, vecs.at[gather.section], local_sem.at[2, 1]),
+    ]
+    for copy in local[0] + tiny + local[1]:
+        copy.start()
+    gather.barrier()
+    for copy in local[0] + tiny:
+        copy.wait()
+    gather.start(0, 0)
+    small = small_copies(gather, adapters, small_sem, 0) + small_copies(gather, vecs, small_sem, 3)
+    for copy in small:
+        copy.start()
+    gather.start(0, 1)
+    gather.spread(0, 0)
+    for copy in local[1]:
+        copy.wait()
+    gather.relay(0, 0)
+    gather.spread(0, 1)
+    gather.close(0, 0)
+    gather.start(1, 0)
+    gather.relay(0, 1)
+    gather.spread(1, 0)
+    gather.start(1, 1)
+    gather.close(0, 1)
+    gather.relay(1, 0)
+    gather.spread(1, 1)
+    gather.close(1, 0)
+    gather.relay(1, 1)
+    gather.close(1, 1)
+    for copy in small:
+        copy.wait()
+    for layer in range(2):
+        for group in range(2):
+            gather.arrive(layer, group)
+            gather.drain(layer, group)
+
+
+def gather_everything(qkv_w, attn_w, in_w, out_w, own_adapter, own_vec):
+    width = qkv_w.shape[2] // 3
+    rows = qkv_w.shape[1]
+    shards = lax.axis_size("dp")
+    sections = lax.axis_size("section")
+    anyspec = pl.BlockSpec(memory_space=pl.ANY)
+    sems = Gather.semaphores(shards // 2)
+    full = jax.ShapeDtypeStruct((shards, 4, 3, rows, width), BF16)
+    return pl.pallas_call(
+        gather_kernel,
+        in_specs=[anyspec] * 6,
+        out_specs=[anyspec] * 4,
+        out_shape=[
+            full, full, jax.ShapeDtypeStruct((sections,) + own_adapter.shape, BF16),
+            jax.ShapeDtypeStruct((sections,) + own_vec.shape, F32),
+        ],
+        scratch_shapes=[
+            sems["z"], sems["side"], sems["corner"], sems["core"], pltpu.SemaphoreType.DMA((2, 6)), pltpu.SemaphoreType.DMA((3, 12)),
+        ],
+        compiler_params=pltpu.CompilerParams(collective_id=1, has_side_effects=True),
+        cost_estimate=pl.CostEstimate(flops=0, bytes_accessed=60_000_000, transcendentals=0),
+        name="gather_weights",
+    )(qkv_w, attn_w, in_w, out_w, own_adapter, own_vec)
+
+
 X_PAIRS = [(0, 1), (1, 0), (2, 3), (3, 2)]
 Y_PAIRS = [(0, 2), (2, 0), (1, 3), (3, 1)]
 CROSS = [(0, 3), (3, 0), (1, 2), (2, 1)]
@@ -496,25 +717,25 @@
             jnp.stack([in_quarters(ffn_in_weight[layer]), outer.reshape((4, -1) + outer.shape[1:])], 1),
         )
 
-    weights = []
-    for layer in range(layers):
-        attn, inner = layer_shards(layer)
-        if layer == 0:
-            attn_full = gather_weights(attn)
-            inner_full = gather_weights(inner)
-            weights.append([block_rows(attn_full, 0, False), block_rows(inner_full, 0, False), block_rows(inner_full, 1, True)])
-        else:
-            full = gather_weights(jnp.concatenate([attn, inner], 1))
+    zero_row = jnp.zeros((1, width), F32)
+    own_vec = jnp.concatenate(
+        [zero_row, up_bias, ln_gain, ln_beta, jnp.pad(down_bias, ((0, 0), (0, width - adapter_width))), zero_row, zero_row, zero_row], 0
+    )
+    own_adapter = jnp.concatenate([down_weight[0].T, up_weight[0]], 0)
+    if lax.axis_size("dp") == 8 and lax.axis_size("section") == 4:
+        full0, full1, adapters, vecs = gather_everything(
+            qkv_weight, attn_out_weight, ffn_in_weight, ffn_out_weight, own_adapter, own_vec
+        )
+        weights = [[(full, kind) for kind in range(3)] for full in (full0, full1)]
+    else:
+        weights = []
+        for layer in range(layers):
+            full = gather_weights(jnp.concatenate(layer_shards(layer), 1))
             weights.append([block_rows(full, 0, False), block_rows(full, 1, False), block_rows(full, 2, True)])
-
-    zero_row = jnp.zeros((1, width), F32)
-    own_vecs = jnp.concatenate(
-        [zero_row, up_bias, ln_gain, ln_beta, jnp.pad(down_bias, ((0, 0), (0, width - adapter_width))), zero_row, zero_row, zero_row], 0
-    )
-    own_pack = jnp.concatenate([down_weight[0].T.astype(F32), up_weight[0].astype(F32), own_vecs], 0)
-    packs = lax.all_gather(own_pack, "section", axis=0, tiled=False)
-    adapters = packs[:, :128].astype(BF16).reshape(layers, 2, 128, width)
-    vecs = packs[:, 128:].reshape(layers, 2, 8, width)
+        adapters = lax.all_gather(own_adapter, "section", axis=0, tiled=False)
+        vecs = lax.all_gather(own_vec, "section", axis=0, tiled=False)
+    adapters = adapters.reshape(layers, 2, 128, width)
+    vecs = vecs.reshape(layers, 2, 8, width)
     vecs = vecs.at[:, 0, 0].set(attn_out_bias).at[:, 0, 5].set(query_bias).at[:, 0, 6].set(value_bias)
     vecs = vecs.at[:, 1, 0].set(ffn_out_bias).reshape(layers, 16, width)
     in_bias = ffn_in_bias[:, None, :]

time: 681 us -> 648 us (0.952)
  waiting for transfers between devices: 336 us -> 131 us
  Pallas kernels: 207 us -> 407 us
  local copies, waits for them, and re-layouts: 41.8 us -> 27.8 us
    all_gather x4 -> x0, waiting for transfers between devices: 224 us -> none  [the longest x3 215 us: gather_weights(): full = lax.all_gather(quarter, ('dp', 'section'), axis=0, tiled=False)]
    pallas_call x0 -> x1, Pallas kernels: none -> 199 us  [gather_everything(): pl.pallas_call(gather_kernel, in_specs=[anyspec] * 6, out_specs=[anyspec]...]
    ppermute x14, waiting for transfers between devices: 57.2 us -> 78.6 us  [send(): lax.ppermute(value, 'section', [pair for pair in pairs if pair[0] in send...]
  transfers between devices with their start and end apart: 20 -> 16, of which waited for: 7 -> 4; matrix products, arithmetic and copies ran while one was open for 11% -> 6% of each run, Pallas kernels for 31% -> 25%
where the time goes in v2:
time: 648 us; the launch traced here: 650 us
  Pallas kernels  407 us (63%)
  waiting for transfers between devices  131 us (20%)
  other arithmetic  40.7 us (6%)
  local copies, waits for them, and re-layouts  27.8 us (4%)
  starting transfers between devices  26.1 us (4%)
  between operations  17.3 us (3%)
    pallas_call x6, Pallas kernels, call_with_weights(): pl.pallas_call(body, grid_spec=pltpu.PrefetchScalarGridSpec(num_scalar_pr...  208 us
    pallas_call x1, Pallas kernels, gather_everything(): pl.pallas_call(gather_kernel, in_specs=[anyspec] * 6, out_specs=[anyspec]...  199 us
    ppermute x14, waiting for transfers between devices, send(): lax.ppermute(value, 'section', [pair for pair in pairs if pair[0] in send...  78.6 us
    psum x1, waiting for transfers between devices, on_device(): total = lax.psum(mine, 'dp')  52.4 us
    ppermute x14, starting transfers between devices, send(): lax.ppermute(value, 'section', [pair for pair in pairs if pair[0] in send...  26 us
    dynamic_update_slice x10, other arithmetic, assemble(): result = lax.dynamic_update_index_in_dim(result, part, row, 0)  13.5 us
  transfers between devices with their start and end apart: 16, of which 4 were waited for; matrix products, arithmetic and copies ran while one was open for 6% of the time, Pallas kernels for 25%

profile of v2, /device:TPU:0, one launch (start us, length us, event | category | flops | bytes accessed | tf_op | source)
XLA Modules:
  0.0 649.6 jit_solution(9584745982482461000)
XLA Ops:
  12.7 2.1 dynamic-slice_bitcast_fusion.1.refs_1_
  18.4 199.0 %gather_weights.1 = (bf16[8,4,3,96,768]{4,3,2,1,0:T(8,128)(2,1)}, bf16[8,4,3,96,768]{4,3,2,1,0:T(8,128)(2,1)}, bf16[4,128,768]{2,1,0:T(8,128)(2,1)}, f32[4,8,768]{2,1,0:T(8,128)}) custom-call(bf16[2,96,2304]{2,1,0:T(8,128)(2,1)} %qkv_w.1, bf16[2,96,768]{2,1,0:T(8,128)(2,1)} %attn_w.1, bf16[2,96,3072]{2,1,0:T(8,128)(2,1)} %in_w.1, ...), custom_call_target="tpu_custom_call" | custom-call | bytes 60000000 | tf_op jit(solution)/shard_map/gather_weights/pallas_call | solution.py:651
  220.3 1.9 constant_dynamic-update-slice_fusion.5
  222.2 1.9 constant_dynamic-update-slice_fusion.4
  225.4 1.9 pad_add_fusion.1
  227.3 43.9 %forward_pair.3 = (bf16[512,768]{1,0:T(8,128)(2,1)}, bf16[512,768]{1,0:T(8,128)(2,1)}, bf16[512,2304]{1,0:T(8,128)(2,1)}, bf16[512,768]{1,0:T(8,128)(2,1)}, bf16...) custom-call(s32[3]{0:T(128)} %get-tuple-element.228.refs_0_, ...), custom_call_target="tpu_custom_call" | custom-call | flops 12000000000 | bytes 24000000 | tf_op jit(solution)/shard_map/forward_pair/pallas_call | solution.py:251
  271.2 2.9 broadcast_select_fusion.10
  275.4 3.4 collective-permute-start.5
  278.8 2.6 collective-permute-start.1
  281.4 32.2 %forward_pair.4 = (bf16[512,768]{1,0:T(8,128)(2,1)}, bf16[512,768]{1,0:T(8,128)(2,1)}, bf16[512,2304]{1,0:T(8,128)(2,1)}, bf16[512,768]{1,0:T(8,128)(2,1)}, bf16...) custom-call(s32[3]{0:T(128)} %get-tuple-element.229.refs_0_, ...), custom_call_target="tpu_custom_call" | custom-call | flops 12000000000 | bytes 24000000 | tf_op jit(solution)/shard_map/forward_pair/pallas_call | solution.py:251
  316.2 2.1 dynamic-slice_bitcast_fusion.refs_1_
  318.2 2.5 broadcast_in_dim.120.clone
  323.1 31.9 %forward_pair.5 = (bf16[512,768]{1,0:T(8,128)(2,1)}, bf16[512,768]{1,0:T(8,128)(2,1)}, bf16[512,2304]{1,0:T(8,128)(2,1)}, bf16[512,768]{1,0:T(8,128)(2,1)}, bf16...) custom-call(s32[3]{0:T(128)} %pad_add_fusion.refs_0_, ...), custom_call_target="tpu_custom_call" | custom-call | flops 12000000000 | bytes 24000000 | tf_op jit(solution)/shard_map/forward_pair/pallas_call | solution.py:251
  354.9 33.3 %backward_pair.3 = (bf16[512,768]{1,0:T(8,128)(2,1)}, bf16[512,768]{1,0:T(8,128)(2,1)}, f32[2,136,768]{2,1,0:T(8,128)}) custom-call(s32[3]{0:T(128)} %pad_add_fusion.refs_0_, bf16[512,768]{1,0:T(8,128)(2,1)} %dynamic-slice_bitcast_fusion.refs_1_, bf16[512,128]{1,0:T(8,128)(2,1)} %get-tuple-element.209.refs_2_, bf16[512,2304]{1,0:T(8,128)(2,1)} %get-tuple-element.152.refs_3_, ...), custom_call_target="tpu_custom_call" | custom-call | flops 16000000000 | bytes 24000000 | tf_op jit(solution)/shard_map/backward_pair/pallas_call | solution.py:251
  388.2 2.9 broadcast_select_fusion.6
  391.7 33.3 %backward_pair.4 = (bf16[512,768]{1,0:T(8,128)(2,1)}, bf16[512,768]{1,0:T(8,128)(2,1)}, f32[2,136,768]{2,1,0:T(8,128)}) custom-call(s32[3]{0:T(128)} %get-tuple-element.229.refs_0_, bf16[512,768]{1,0:T(8,128)(2,1)} %get-tuple-element.205.refs_1_, bf16[512,128]{1,0:T(8,128)(2,1)} %get-tuple-element.210.refs_2_, bf16[512,2304]{1,0:T(8,128)(2,1)} %get-tuple-element.162.refs_3_, ...), custom_call_target="tpu_custom_call" | custom-call | flops 16000000000 | bytes 24000000 | tf_op jit(solution)/shard_map/backward_pair/pallas_call | solution.py:251
  426.5 2.7 broadcast_select_fusion.4
  429.2 33.1 %backward_pair.5 = (bf16[512,768]{1,0:T(8,128)(2,1)}, bf16[512,768]{1,0:T(8,128)(2,1)}, f32[2,136,768]{2,1,0:T(8,128)}) custom-call(s32[3]{0:T(128)} %get-tuple-element.228.refs_0_, bf16[512,768]{1,0:T(8,128)(2,1)} %get-tuple-element.206.refs_1_, bf16[512,128]{1,0:T(8,128)(2,1)} %get-tuple-element.211.refs_2_, bf16[512,2304]{1,0:T(8,128)(2,1)} %get-tuple-element.174.refs_3_, ...), custom_call_target="tpu_custom_call" | custom-call | flops 16000000000 | bytes 24000000 | tf_op jit(solution)/shard_map/backward_pair/pallas_call | solution.py:251
  465.9 4.1 collective-permute-start.2
  470.0 2.0 collective-permute-start.4
  472.0 2.5 broadcast_in_dim.120.clone.1
  476.5 2.1 bitcast_dynamic-update-slice_fusion.10
  479.5 33.6 %collective-permute-done.2 = bf16[512,768]{1,0:T(8,128)(2,1)S(1)} collective-permute-done((bf16[512,768]{1,0:T(8,128)(2,1)S(1)}, bf16[512,768]{1,0:T(8,128)(2,1)S(1)}, u32[]{:S(2)}, u32[]{:S(2)}) %collective-permute-start.2) | collective-permute-done | bytes 786464 | tf_op jit(solution)/shard_map/ppermute | solution.py:674
  513.1 3.3 collective-permute-start.11
  518.9 2.6 collective-permute-start.7
  521.5 2.2 bitcast_dynamic-update-slice_fusion.8
  527.2 2.2 bitcast_dynamic-update-slice_fusion.6
  529.4 28.1 %collective-permute-done.7 = bf16[512,768]{1,0:T(8,128)(2,1)S(1)} collective-permute-done((bf16[512,768]{1,0:T(8,128)(2,1)S(1)}, bf16[512,768]{1,0:T(8,128)(2,1)S(1)}, u32[]{:S(2)}, u32[]{:S(2)}) %collective-permute-start.7) | collective-permute-done | bytes 786464 | tf_op jit(solution)/shard_map/ppermute | solution.py:674
  557.5 1.9 collective-permute-start.12
  561.5 16.8 %collective-permute-done.10 = bf16[512,768]{1,0:T(8,128)(2,1)S(1)} collective-permute-done((bf16[512,768]{1,0:T(8,128)(2,1)}, bf16[512,768]{1,0:T(8,128)(2,1)S(1)}, u32[]{:S(2)}, u32[]{:S(2)}) %collective-permute-start.10) | collective-permute-done | bytes 786464 | tf_op jit(solution)/shard_map/ppermute | solution.py:674
  581.9 52.4 %all-reduce.4.cloned.1.call-done = f32[136,768]{1,0:T(8,128)} async-done(((f32[136,768]{1,0:T(8,128)}), f32[136,768]{1,0:T(8,128)}) %all-reduce.4.cloned.1.call-update) | async-done | bytes 417808 | tf_op jit(solution)/shard_map/psum | solution.py:831
  636.9 1.8 slice_bitcast_fusion
  (120 shorter events, 43.1 us)
Async XLA Ops:
  7.2 212.4 %copy-start.22 = (s32[4]{0:T(128)S(1)}, s32[4]{0:T(128)}, u32[]{:S(2)}) copy-start(s32[4]{0:T(128)} %constant.322.clone.1) | copy-start | bytes 52
  7.2 213.1 %copy-start.18 = (f32[2,768]{1,0:T(2,128)S(1)}, f32[2,768]{1,0:T(2,128)}, u32[]{:S(2)}) copy-start(f32[2,768]{1,0:T(2,128)} %param.47) | copy-start | bytes 18436
  7.2 213.1 %copy-start.20 = (f32[2,768]{1,0:T(2,128)S(1)}, f32[2,768]{1,0:T(2,128)}, u32[]{:S(2)}) copy-start(f32[2,768]{1,0:T(2,128)} %param.44) | copy-start | bytes 18436
  7.2 215.0 %copy-start.21 = (f32[2,768]{1,0:T(2,128)S(1)}, f32[2,768]{1,0:T(2,128)}, u32[]{:S(2)}) copy-start(f32[2,768]{1,0:T(2,128)} %param.45) | copy-start | bytes 18436
  7.2 216.9 %copy-start.19 = (f32[2,768]{1,0:T(2,128)S(1)}, f32[2,768]{1,0:T(2,128)}, u32[]{:S(2)}) copy-start(f32[2,768]{1,0:T(2,128)} %param.51) | copy-start | bytes 18436
  7.2 217.6 %copy-start.15 = (f32[2,3072]{1,0:T(2,128)S(1)}, f32[2,3072]{1,0:T(2,128)}, u32[]{:S(2)}) copy-start(f32[2,3072]{1,0:T(2,128)} %param.49) | copy-start | bytes 73732
  7.2 573.5 %reduce-scatter.4.cloned.1.call-start = ((), (), s32[]{:S(2)}) async-start(), calls=%async_computation.2 | async-start | bytes 2088960
  274.1 243.5 %collective-permute-start.3 = (bf16[512,768]{1,0:T(8,128)(2,1)}, bf16[512,768]{1,0:T(8,128)(2,1)}, u32[]{:S(2)}, u32[]{:S(2)}) collective-permute-start(bf16[512,768]{1,0:T(8,128)(2,1)} %get-tuple-element.201), channel_id=1, source_target_pairs={{24,0},{16,8},{25,1},{17,9},{26,2},{18,10},{27,3},{19,11},{28,4},{... | collective-permute-start | bytes 2359304 | tf_op jit(solution)/shard_map/ppermute | solution.py:674
  275.4 249.6 %collective-permute-start.5 = (bf16[512,768]{1,0:T(8,128)(2,1)}, bf16[512,768]{1,0:T(8,128)(2,1)}, u32[]{:S(2)}, u32[]{:S(2)}) collective-permute-start(bf16[512,768]{1,0:T(8,128)(2,1)} %get-tuple-element.201), channel_id=1, source_target_pairs={{0,8},{8,0},{1,9},{9,1},{2,10},{10,2},{3,11},{11,3},{4,12},{12,4},... | collective-permute-start | bytes 2359304 | tf_op jit(solution)/shard_map/ppermute | solution.py:674
  278.8 43.0 %collective-permute-start.1 = (bf16[512,768]{1,0:T(8,128)(2,1)S(1)}, bf16[512,768]{1,0:T(8,128)(2,1)S(1)}, u32[]{:S(2)}, u32[]{:S(2)}) collective-permute-start(bf16[512,768]{1,0:T(8,128)(2,1)S(1)} %get-tuple-element.202), channel_id=1, source_target_pairs={{0,16},{16,0},{8,24},{24,8},{1,17},{17,1},{9,25},{25,9},{2,18},{18... | collective-permute-start | bytes 2359304 | tf_op jit(solution)/shard_map/ppermute | solution.py:674
  281.4 33.3 %copy-start.16 = (f32[8,768]{1,0:T(8,128)S(1)}, f32[8,768]{1,0:T(8,128)}, u32[]{:S(2)}) copy-start(f32[8,768]{1,0:T(8,128)} %get-tuple-element.186) | copy-start | bytes 73732
  391.1 35.4 %collective-permute-start.8 = (bf16[512,768]{1,0:T(8,128)(2,1)S(1)}, bf16[512,768]{1,0:T(8,128)(2,1)S(1)}, u32[]{:S(2)}, u32[]{:S(2)}) collective-permute-start(bf16[512,768]{1,0:T(8,128)(2,1)S(1)} %get-tuple-element.196), channel_id=1, source_target_pairs={{0,16},{16,0},{8,24},{24,8},{1,17},{17,1},{9,25},{25,9},{2,18},{18... | collective-permute-start | bytes 2359304 | tf_op jit(solution)/shard_map/ppermute | solution.py:674
  391.1 84.5 %collective-permute-start = (bf16[512,768]{1,0:T(8,128)(2,1)}, bf16[512,768]{1,0:T(8,128)(2,1)}, u32[]{:S(2)}, u32[]{:S(2)}) collective-permute-start(bf16[512,768]{1,0:T(8,128)(2,1)} %get-tuple-element.213), channel_id=1, source_target_pairs={{0,8},{8,0},{16,24},{24,16},{1,9},{9,1},{17,25},{25,17},{2,10},{10... | collective-permute-start | bytes 2359304 | tf_op jit(solution)/shard_map/ppermute | solution.py:674
  391.7 33.3 %copy-start.17 = (f32[8,768]{1,0:T(8,128)S(1)}, f32[8,768]{1,0:T(8,128)}, u32[]{:S(2)}) copy-start(f32[8,768]{1,0:T(8,128)} %get-tuple-element.190) | copy-start | bytes 73732
  429.2 33.9 %copy-start.12 = (f32[2,136,768]{2,1,0:T(8,128)S(1)}, f32[2,136,768]{2,1,0:T(8,128)}, u32[]{:S(2)}) copy-start(f32[2,136,768]{2,1,0:T(8,128)} %constant_dynamic-update-slice_fusion) | copy-start | bytes 2506756
  429.2 33.9 %copy-start.13 = (f32[2,136,768]{2,1,0:T(8,128)S(1)}, f32[2,136,768]{2,1,0:T(8,128)}, u32[]{:S(2)}) copy-start(f32[2,136,768]{2,1,0:T(8,128)} %constant_dynamic-update-slice_fusion.1) | copy-start | bytes 2506756
  465.7 168.6 %all-reduce.4.cloned.1.call-start = ((), (), s32[]{:S(2)}) async-start(), calls=%async_computation.1 | async-start | bytes 835584 | tf_op jit(solution)/shard_map/psum | solution.py:831
  465.9 12.6 %copy-start.2 = (bf16[512,768]{1,0:T(8,128)(2,1)S(1)}, bf16[512,768]{1,0:T(8,128)(2,1)}, u32[]{:S(2)}) copy-start(bf16[512,768]{1,0:T(8,128)(2,1)} %get-tuple-element.183) | copy-start | bytes 2359300
  465.9 47.2 %collective-permute-start.2 = (bf16[512,768]{1,0:T(8,128)(2,1)S(1)}, bf16[512,768]{1,0:T(8,128)(2,1)S(1)}, u32[]{:S(2)}, u32[]{:S(2)}) collective-permute-start(bf16[512,768]{1,0:T(8,128)(2,1)S(1)} %get-tuple-element.200), channel_id=1, source_target_pairs={{0,16},{8,24},{1,17},{9,25},{2,18},{10,26},{3,19},{11,27},{4,20},{... | collective-permute-start | bytes 2359304 | tf_op jit(solution)/shard_map/ppermute | solution.py:674
  470.0 48.8 %collective-permute-start.4 = (bf16[512,768]{1,0:T(8,128)(2,1)S(1)}, bf16[512,768]{1,0:T(8,128)(2,1)S(1)}, u32[]{:S(2)}, u32[]{:S(2)}) collective-permute-start(bf16[512,768]{1,0:T(8,128)(2,1)S(1)} %get-tuple-element.199), channel_id=1, source_target_pairs={{0,24},{8,16},{1,25},{9,17},{2,26},{10,18},{3,27},{11,19},{4,28},{... | collective-permute-start | bytes 2359304 | tf_op jit(solution)/shard_map/ppermute | solution.py:674
  474.5 44.3 %copy-start.14 = (bf16[512,768]{1,0:T(8,128)(2,1)S(1)}, bf16[512,768]{1,0:T(8,128)(2,1)}, u32[]{:S(2)}) copy-start(bf16[512,768]{1,0:T(8,128)(2,1)} %get-tuple-element.207) | copy-start | bytes 2359300
  475.6 48.1 %copy-start.8 = (bf16[512,768]{1,0:T(8,128)(2,1)S(1)}, bf16[512,768]{1,0:T(8,128)(2,1)}, u32[]{:S(2)}) copy-start(bf16[512,768]{1,0:T(8,128)(2,1)} %get-tuple-element.149) | copy-start | bytes 2359300
  475.6 48.1 %copy-start.9 = (bf16[512,768]{1,0:T(8,128)(2,1)S(1)}, bf16[512,768]{1,0:T(8,128)(2,1)}, u32[]{:S(2)}) copy-start(bf16[512,768]{1,0:T(8,128)(2,1)} %get-tuple-element.145) | copy-start | bytes 2359300
  475.6 50.2 %collective-permute-start.6 = (bf16[512,768]{1,0:T(8,128)(2,1)S(1)}, bf16[512,768]{1,0:T(8,128)(2,1)S(1)}, u32[]{:S(2)}, u32[]{:S(2)}) collective-permute-start(bf16[512,768]{1,0:T(8,128)(2,1)S(1)} %get-tuple-element.199), channel_id=1, source_target_pairs={{16,24},{24,16},{17,25},{25,17},{18,26},{26,18},{19,27},{27,19},{2... | collective-permute-start | bytes 2359304 | tf_op jit(solution)/shard_map/ppermute | solution.py:674
  513.1 48.3 %collective-permute-start.11 = (bf16[512,768]{1,0:T(8,128)(2,1)}, bf16[512,768]{1,0:T(8,128)(2,1)S(1)}, u32[]{:S(2)}, u32[]{:S(2)}) collective-permute-start(bf16[512,768]{1,0:T(8,128)(2,1)} %get-tuple-element.195), channel_id=1, source_target_pairs={{0,24},{8,16},{1,25},{9,17},{2,26},{10,18},{3,27},{11,19},{4,28},{... | collective-permute-start | bytes 2359304 | tf_op jit(solution)/shard_map/ppermute | solution.py:674
  517.6 42.8 %collective-permute-start.9 = (bf16[512,768]{1,0:T(8,128)(2,1)S(1)}, bf16[512,768]{1,0:T(8,128)(2,1)S(1)}, u32[]{:S(2)}, u32[]{:S(2)}) collective-permute-start(bf16[512,768]{1,0:T(8,128)(2,1)S(1)} %get-tuple-element.198), channel_id=1, source_target_pairs={{16,0},{24,8},{17,1},{25,9},{18,2},{26,10},{19,3},{27,11},{20,4},{... | collective-permute-start | bytes 2359304 | tf_op jit(solution)/shard_map/ppermute | solution.py:674
  518.9 38.7 %collective-permute-start.7 = (bf16[512,768]{1,0:T(8,128)(2,1)S(1)}, bf16[512,768]{1,0:T(8,128)(2,1)S(1)}, u32[]{:S(2)}, u32[]{:S(2)}) collective-permute-start(bf16[512,768]{1,0:T(8,128)(2,1)S(1)} %copy-done.14), channel_id=1, source_target_pairs={{0,8},{8,0},{16,24},{24,16},{1,9},{9,1},{17,25},{25,17},{2,10},{10... | collective-permute-start | bytes 2359304 | tf_op jit(solution)/shard_map/ppermute | solution.py:674
  525.0 54.4 %copy-start.10 = (bf16[512,768]{1,0:T(8,128)(2,1)S(1)}, bf16[512,768]{1,0:T(8,128)(2,1)}, u32[]{:S(2)}) copy-start(bf16[512,768]{1,0:T(8,128)(2,1)} %get-tuple-element.173) | copy-start | bytes 2359300
  525.0 54.4 %copy-start.11 = (bf16[512,768]{1,0:T(8,128)(2,1)S(1)}, bf16[512,768]{1,0:T(8,128)(2,1)}, u32[]{:S(2)}) copy-start(bf16[512,768]{1,0:T(8,128)(2,1)} %get-tuple-element.161) | copy-start | bytes 2359300
  525.0 55.8 %collective-permute-start.13 = (bf16[512,768]{1,0:T(8,128)(2,1)}, bf16[512,768]{1,0:T(8,128)(2,1)S(1)}, u32[]{:S(2)}, u32[]{:S(2)}) collective-permute-start(bf16[512,768]{1,0:T(8,128)(2,1)} %get-tuple-element.195), channel_id=1, source_target_pairs={{16,24},{24,16},{17,25},{25,17},{18,26},{26,18},{19,27},{27,19},{2... | collective-permute-start | bytes 2359304 | tf_op jit(solution)/shard_map/ppermute | solution.py:674
  525.9 52.5 %collective-permute-start.10 = (bf16[512,768]{1,0:T(8,128)(2,1)}, bf16[512,768]{1,0:T(8,128)(2,1)S(1)}, u32[]{:S(2)}, u32[]{:S(2)}) collective-permute-start(bf16[512,768]{1,0:T(8,128)(2,1)} %get-tuple-element.197), channel_id=1, source_target_pairs={{24,0},{16,8},{25,1},{17,9},{26,2},{18,10},{27,3},{19,11},{28,4},{... | collective-permute-start | bytes 2359304 | tf_op jit(solution)/shard_map/ppermute | solution.py:674
  557.5 23.2 %collective-permute-start.12 = (bf16[512,768]{1,0:T(8,128)(2,1)}, bf16[512,768]{1,0:T(8,128)(2,1)S(1)}, u32[]{:S(2)}, u32[]{:S(2)}) collective-permute-start(bf16[512,768]{1,0:T(8,128)(2,1)} %get-tuple-element.197), channel_id=1, source_target_pairs={{0,8},{8,0},{1,9},{9,1},{2,10},{10,2},{3,11},{11,3},{4,12},{12,4},... | collective-permute-start | bytes 2359304 | tf_op jit(solution)/shard_map/ppermute | solution.py:674
  (7 other events, 51.2 us)
Sparse Core Ops, SparseCore 0:
  465.8 66.7 reduce-scatter.3
  580.9 53.3 all-reduce.3

commit v3 on v1

--- a/solution.py
+++ b/solution.py
@@ -444,6 +444,657 @@
     return table.astype(BF16)
 
 
+MESH = pl.DeviceIdType.MESH
+GRAD_ROWS = 144
+MEGA_BYTES = 63 * 1024 * 1024
+
+
+def when(condition, action):
+    if condition is None:
+        action()
+    else:
+        pl.when(condition)(action)
+
+
+class Place:
+    def __init__(self):
+        self.section = lax.axis_index("section")
+        self.dp = lax.axis_index("dp")
+        self.count = lax.axis_size("dp") // 2
+        self.z = self.dp // 2
+        self.core = self.dp % 2
+        self.side = self.section % 2
+        self.early = self.section < 2
+        self.late = self.section >= 2
+        self.x_side = self.section + 1 - 2 * self.side
+        self.y_side = lax.rem(self.section + 2, 4)
+        self.corner = 3 - self.section
+        self.to_x = (self.x_side, self.dp)
+        self.to_y = (self.y_side, self.dp)
+        self.to_corner = (self.corner, self.dp)
+        self.to_core = (self.section, self.dp + 1 - 2 * self.core)
+
+    def to_z(self, step):
+        return (self.section, lax.rem(self.z + step, self.count) * 2 + self.core)
+
+    def from_z(self, step):
+        return lax.rem(self.z + self.count - step, self.count) * 2 + self.core
+
+    def peers(self):
+        return [self.to_z(d) for d in range(1, self.count)] + [self.to_x, self.to_y, self.to_corner, self.to_core]
+
+    def barrier(self):
+        entry = pltpu.get_barrier_semaphore()
+        for peer in self.peers():
+            pl.semaphore_signal(entry, inc=1, device_id=peer, device_id_type=MESH)
+        pl.semaphore_wait(entry, len(self.peers()))
+
+
+def remote(src, dst, send_sem, recv_sem, device):
+    return pltpu.make_async_remote_copy(
+        src_ref=src, dst_ref=dst, send_sem=send_sem, recv_sem=recv_sem, device_id=device, device_id_type=MESH
+    )
+
+
+class Gather:
+    def __init__(self, full, sems, place):
+        self.full = full
+        self.sems = sems
+        self.place = place
+        self.steps = range(1, place.count)
+
+    def copy(self, unit, shard, quarter, rows, name, spot, device):
+        ref = self.full.at[unit // 3, shard, quarter, unit % 3]
+        ref = ref if rows is None else ref.at[rows]
+        spot = (unit,) + spot
+        return remote(ref, ref, self.sems[name].at[(0,) + spot], self.sems[name].at[(1,) + spot], device)
+
+    def z_copy(self, unit, step):
+        at = self.place
+        return self.copy(unit, at.dp, at.section, None, "z", (step - 1,), at.to_z(step))
+
+    def side_copy(self, unit, step, way):
+        at = self.place
+        return self.copy(unit, at.from_z(step), at.section, None, "side", (step - 1, way), (at.to_x, at.to_y)[way])
+
+    def corner_copy(self, unit, step, way):
+        at = self.place
+        half = self.full.shape[4] // 2
+        quarter, target = (at.x_side, at.to_y) if way == 0 else (at.y_side, at.to_x)
+        return self.copy(unit, at.from_z(step), quarter, pl.ds(way * half, half), "corner", (step - 1, way), target)
+
+    def core_copy(self, unit, step, which):
+        at = self.place
+        quarter = (at.section, at.x_side, at.y_side, at.corner)[which]
+        return self.copy(unit, at.from_z(step), quarter, None, "core", (step, which), at.to_core)
+
+    def begin(self, unit):
+        for step in self.steps:
+            self.z_copy(unit, step).start()
+        for which in range(4):
+            self.core_copy(unit, 0, which).start()
+
+    def spread(self, unit):
+        for step in self.steps:
+            self.z_copy(unit, step).wait_recv()
+            for way in range(2):
+                self.side_copy(unit, step, way).start()
+            self.core_copy(unit, step, 0).start()
+
+    def relay(self, unit):
+        for step in self.steps:
+            for way in range(2):
+                self.side_copy(unit, step, way).wait_recv()
+                self.corner_copy(unit, step, way).start()
+                self.core_copy(unit, step, 1 + way).start()
+
+    def close(self, unit):
+        for step in self.steps:
+            for way in range(2):
+                self.corner_copy(unit, step, way).wait_recv()
+            self.core_copy(unit, step, 3).start()
+
+    def arrive(self, unit):
+        for step in range(self.place.count):
+            for which in range(4):
+                self.core_copy(unit, step, which).wait_recv()
+
+    def drain(self, unit):
+        for step in self.steps:
+            self.z_copy(unit, step).wait_send()
+            for way in range(2):
+                self.side_copy(unit, step, way).wait_send()
+                self.corner_copy(unit, step, way).wait_send()
+        for step in range(self.place.count):
+            for which in range(4):
+                self.core_copy(unit, step, which).wait_send()
+
+
+class Rows:
+    def __init__(self, place, done, results, mail, send_sems, recv_sems, local_sems):
+        self.place = place
+        self.done = done
+        self.send_sems = send_sems
+        self.recv_sems = recv_sems
+        self.local_sems = local_sems
+        self.moves = []
+        self.locals = []
+        at = place
+        own = at.section
+        shared = 4 + at.side
+        other = 1 - at.side
+        early, late = at.early, at.late
+        for step in range(6):
+            out = results[step // 3]
+            kind = step if step < 3 else 5 - step
+            if kind == 1:
+                moves = [(None, None, other, out.at[own], at.to_x)]
+                local = (None, out.at[own])
+            elif kind == 0:
+                moves = [
+                    (early, early, other, out.at[shared], at.to_x),
+                    (late, early, at.side, out.at[own], at.to_y),
+                    (late, early, other, out.at[own], at.to_corner),
+                ]
+                local = (early, out.at[shared])
+            else:
+                moves = [
+                    (late, late, other, out.at[shared], at.to_x),
+                    (early, late, at.side, out.at[own], at.to_y),
+                    (early, late, other, out.at[own], at.to_corner),
+                ]
+                local = (late, out.at[shared])
+            if step == 0:
+                moves.insert(0, (early, late, 1, mail.at[2], at.to_y))
+            if step == 3:
+                moves.insert(0, (late, early, 0, mail.at[3], at.to_y))
+            self.moves.append(moves)
+            self.locals.append(local)
+
+    def make(self, step, number):
+        _, _, pick, target, device = self.moves[step][number]
+        src = self.done.at[2 * (step % 3) + pick]
+        return remote(src, target, self.send_sems.at[step, number], self.recv_sems.at[step, number], device)
+
+    def make_local(self, step):
+        src = self.done.at[2 * (step % 3) + self.place.side]
+        return pltpu.make_async_copy(src, self.locals[step][1], self.local_sems.at[step])
+
+    def ready(self, step, which):
+        for number, (sends, _, pick, _, _) in enumerate(self.moves[step]):
+            if isinstance(pick, int):
+                if pick == which:
+                    when(sends, self.make(step, number).start)
+            else:
+                chosen = pick == which
+                when(chosen if sends is None else sends & chosen, self.make(step, number).start)
+        sends = self.locals[step][0]
+        chosen = self.place.side == which
+        when(chosen if sends is None else sends & chosen, self.make_local(step).start)
+
+    def sent(self, step):
+        for number, (sends, *_) in enumerate(self.moves[step]):
+            when(sends, self.make(step, number).wait_send)
+        when(self.locals[step][0], self.make_local(step).wait)
+
+    def mail_here(self, step):
+        when(self.moves[step][0][1], self.make(step, 0).wait_recv)
+
+    def received(self, step):
+        for number, (_, receives, *_) in enumerate(self.moves[step]):
+            if step in (0, 3) and number == 0:
+                continue
+            when(receives, self.make(step, number).wait_recv)
+
+
+def mega_kernel(
+    inputs, cotangent, table, qkv_w, attn_w, in_w, out_w, own_adapter, own_vec, biases, in_bias,
+    outputs, input_grads, full, spill, result,
+    attn_v, in_v, out_v, qkv, att, branches, norms, aux, slope, hid, keyb, done, acc, low, dqkv,
+    adapters, vecs, grads, parts, total, halves, final,
+    z_sem, side_sem, corner_sem, core_sem, own_sem, small_sem, load_sem, row_send, row_recv, row_local, misc_sem,
+    part_sem, half_sem,
+):
+    at = Place()
+    length, width = hid.shape[1:]
+    chunks = in_v.shape[0]
+    cols = [pl.ds(c * width, width) for c in range(chunks)]
+    gather = Gather(full, {"z": z_sem, "side": side_sem, "corner": corner_sem, "core": core_sem}, at)
+    rows = Rows(at, done, (outputs, input_grads), hid, row_send, row_recv, row_local)
+    own = at.section
+    shared = 4 + at.side
+    early_one = jnp.where(at.early, 1, 0)
+    first_row = jnp.where(at.early, shared, own)
+    third_row = jnp.where(at.early, own, shared)
+    middle = 1 - early_one
+    layer_of = [0, middle, 1, 1, middle, 0]
+
+    local = [[], []]
+    for layer in range(2):
+        block_rows_ = full.shape[4]
+        for quarter in range(4):
+            first = qkv_w.at[layer, :, cols[quarter]] if quarter < 3 else attn_w.at[layer]
+            slab = out_w.at[layer, pl.ds(quarter * block_rows_, block_rows_)]
+            for kind, source in enumerate((first, in_w.at[layer, :, cols[quarter]], slab)):
+                target = full.at[layer, at.dp, quarter, kind]
+                local[layer].append(pltpu.make_async_copy(source, target, own_sem.at[layer, quarter, kind]))
+    small = [
+        pltpu.make_async_copy(own_adapter, adapters.at[own], misc_sem.at[0]),
+        pltpu.make_async_copy(own_vec, vecs.at[own], misc_sem.at[1]),
+    ]
+    row_in = pltpu.make_async_copy(inputs.at[first_row], hid.at[0], misc_sem.at[2])
+    row_own = pltpu.make_async_copy(inputs.at[own], hid.at[1], misc_sem.at[3])
+    keys_in = [
+        pltpu.make_async_copy(table.at[row], keyb.at[k], misc_sem.at[4 + k])
+        for k, row in enumerate((first_row, own, third_row))
+    ]
+    cot_third = pltpu.make_async_copy(cotangent.at[third_row], hid.at[0], misc_sem.at[7])
+    cot_own = pltpu.make_async_copy(cotangent.at[own], hid.at[1], misc_sem.at[8])
+    spills = [pltpu.make_async_copy(slope, spill.at[k], misc_sem.at[9 + k]) for k in range(2)]
+    returns = [pltpu.make_async_copy(spill.at[k], slope, misc_sem.at[11 + k]) for k in range(2)]
+    for copy in local[0] + small + [row_in] + keys_in + local[1]:
+        copy.start()
+    pl.when(at.early)(row_own.start)
+    grads[...] = jnp.zeros_like(grads)
+    at.barrier()
+    for copy in local[0]:
+        copy.wait()
+    gather.begin(0)
+    for copy in small:
+        copy.wait()
+    shares = []
+    for which, ref in enumerate((adapters, vecs)):
+        for i, device in enumerate((at.to_x, at.to_y, at.to_corner)):
+            spot = 3 * which + i
+            shares.append(remote(ref.at[own], ref.at[own], small_sem.at[0, spot], small_sem.at[1, spot], device))
+    for copy in shares:
+        copy.start()
+    for copy in local[1]:
+        copy.wait()
+
+    tasks = []
+    for name, unit in (
+        ("begin", 1), ("spread", 0), ("begin", 2), ("relay", 0), ("spread", 1), ("begin", 3), ("close", 0),
+        ("relay", 1), ("spread", 2), ("begin", 4), ("close", 1), ("relay", 2), ("spread", 3), ("begin", 5), ("close", 2),
+        ("relay", 3), ("spread", 4), ("close", 3), ("relay", 4), ("spread", 5), ("close", 4), ("relay", 5), ("close", 5),
+    ):
+        tasks.append((name, unit))
+
+    def take(count):
+        chosen = tasks[:count]
+        del tasks[:count]
+
+        def action():
+            for name, unit in chosen:
+                getattr(gather, name)(unit)
+
+        return action
+
+    def tasks_through(unit):
+        if ("close", unit) in tasks:
+            take(tasks.index(("close", unit)) + 1)()
+
+    def load(kinds, layer, start=True):
+        made = []
+        for c in range(chunks):
+            for kind in kinds:
+                if kind < 2:
+                    source, target = full.at[layer, :, c, kind], (attn_v, in_v)[kind].at[c]
+                else:
+                    span = out_v.shape[1]
+                    source, target = full.at[layer, pl.ds(c * span, span), :, kind], out_v.at[c]
+                made.append(pltpu.make_async_copy(source, target, load_sem.at[kind, c]))
+        if start:
+            for copy in made:
+                copy.start()
+
+    def loaded(kind, c):
+        source = full.at[0, :, c, kind] if kind < 2 else full.at[0, pl.ds(0, out_v.shape[1]), :, kind]
+        target = (attn_v, in_v, out_v)[kind].at[c]
+        pltpu.make_async_copy(source, target, load_sem.at[kind, c]).wait()
+
+    def vec(stage, row):
+        return vecs[stage, row : row + 1]
+
+    def bias(stage, row):
+        return biases[stage, row : row + 1]
+
+    def adapter_part(stage, k, sub, hidden, branch):
+        down_t = adapters[stage, :64]
+        lift = adapters[stage, 64:]
+        branch_low = branch.astype(BF16)
+        branches[k, sub] = branch_low
+        down = dot_nt(branch_low, down_t) + vec(stage, 4)[:, :64]
+        act, _ = gelu_both(down)
+        lifted = dot(act.astype(BF16), lift) + vec(stage, 1)
+        hidden_float = hidden.astype(F32)
+        resid = hidden_float + branch + lifted
+        center = resid - jnp.mean(resid, -1, keepdims=True)
+        inverse = lax.rsqrt(jnp.mean(center * center, -1, keepdims=True) + EPSILON)
+        normed = center * inverse
+        norms[k, sub] = normed.astype(BF16)
+        done[2 * k + sub] = (normed * vec(stage, 2) + vec(stage, 3)).astype(BF16)
+        valid = keyb[k, :, 16:17].astype(F32)
+        grads[stage, 132:133] += jnp.sum(lifted * lifted * valid, 0, keepdims=True)
+        grads[stage, 133:134] += jnp.sum(hidden_float * hidden_float * valid, 0, keepdims=True)
+        held = aux.at[k, sub]
+        held[:, :64] = down
+        held[...] = jnp.where(lanes(length) == 64, inverse, held[...])
+
+    def heads(pair, hooks):
+        def body(p, carry):
+            pair(p)
+            for i, hook in enumerate(hooks):
+                pl.when(p == i)(hook)
+            return carry
+
+        lax.fori_loop(0, HEADS // 2, body, 0)
+
+    def attention_forward(k, source, hooks):
+        layer = layer_of[k]
+        stage = 2 * layer
+        hidden = hid[source]
+        for part in range(3):
+            loaded(0, part)
+            mixed = dot(hidden, square(attn_v, part))
+            if part != 1:
+                mixed = mixed + bias(stage, 5 if part == 0 else 6)
+            qkv[k, :, cols[part]] = mixed.astype(BF16)
+        aux[k, 0] = jnp.zeros((length, 128), F32)
+
+        def pair(p):
+            attention_pair_forward(p, 0, length, qkv.at[k], keyb.at[k], att.at[k], aux.at[k, 0])
+
+        heads(pair, hooks)
+        loaded(0, 3)
+        branch = dot(att[k], square(attn_v, 3)) + bias(stage, 0)
+        adapter_part(stage, k, 0, hid[source], branch)
+        rows.ready(k, 0)
+
+    def ffn_forward(k, hooks):
+        layer = layer_of[k]
+        stage = 2 * layer + 1
+        for c in range(chunks):
+            loaded(1, c)
+            pre = dot(done[2 * k], square(in_v, c)) + in_bias[layer, :, c * width : (c + 1) * width]
+            act, steep = gelu_both(pre)
+            slope[:, cols[c]] = steep.astype(BF16)
+            loaded(2, c)
+            term = dot(act.astype(BF16), square(out_v, c))
+            if c == 0:
+                acc[...] = term + bias(stage, 0)
+            else:
+                acc[...] += term
+            if c < len(hooks):
+                hooks[c]()
+        aux[k, 1] = jnp.zeros((length, 128), F32)
+        adapter_part(stage, k, 1, done[2 * k], acc[...])
+        rows.ready(k, 1)
+
+    def adapter_back(stage, k, sub, grad):
+        down_t = adapters[stage, :64]
+        lift = adapters[stage, 64:]
+        grad = grad.astype(F32)
+        normed = norms[k, sub].astype(F32)
+        held = aux[k, sub]
+        inverse = held[:, 64:65]
+        down = held[:, :64]
+        scaled = grad * vec(stage, 2)
+        resid = inverse * (
+            scaled
+            - jnp.mean(scaled, -1, keepdims=True)
+            - normed * jnp.mean(scaled * normed, -1, keepdims=True)
+        )
+        lift_grad = resid.astype(BF16)
+        act, steep = gelu_both(down)
+        down_grad = (dot_nt(lift_grad, lift) * steep).astype(BF16)
+        grads[stage, 0:64] += dot_tn(act.astype(BF16), lift_grad)
+        grads[stage, 64:128] += dot_tn(down_grad, branches[k, sub])
+        grads[stage, 128:129] += jnp.sum(lift_grad.astype(F32), 0, keepdims=True)
+        grads[stage, 129:130] += jnp.sum(normed * grad, 0, keepdims=True)
+        grads[stage, 130:131] += jnp.sum(grad, 0, keepdims=True)
+        grads[stage, 131:132, :64] += jnp.sum(down_grad.astype(F32), 0, keepdims=True)
+        acc[...] = resid
+        low[...] = (resid + dot(down_grad, down_t)).astype(BF16)
+
+    def ffn_backward(step, source, after_adapter):
+        k = 5 - step
+        layer = layer_of[step]
+        adapter_back(2 * layer + 1, k, 1, hid[source])
+        after_adapter()
+        for c in range(chunks):
+            if step > 3:
+                loaded(2, c)
+            act_grad = dot_nt(low[...], square(out_v, c))
+            pre_grad = (act_grad * slope[:, cols[c]].astype(F32)).astype(BF16)
+            if step > 3:
+                loaded(1, c)
+            acc[...] += dot_nt(pre_grad, square(in_v, c))
+        spot = 2 * (step - 3)
+        done[spot + 1] = acc[...].astype(BF16)
+        rows.ready(step, 1)
+
+    def attention_backward(step, after_adapter, hooks):
+        k = 5 - step
+        layer = layer_of[step]
+        spot = 2 * (step - 3)
+        adapter_back(2 * layer, k, 0, done[spot + 1])
+        after_adapter()
+        if step > 3:
+            loaded(0, 3)
+        low[...] = dot_nt(low[...], square(attn_v, 3)).astype(BF16)
+
+        def pair(p):
+            attention_pair_backward(p, 0, length, qkv.at[k], keyb.at[k], att.at[k], aux.at[k, 0], low, dqkv)
+
+        heads(pair, hooks)
+        for part in range(3):
+            if step > 3:
+                loaded(0, part)
+            acc[...] += dot_nt(dqkv[:, cols[part]], square(attn_v, part))
+        done[spot] = acc[...].astype(BF16)
+        rows.ready(step, 0)
+
+    def part_copy(slot, stage, device):
+        return remote(grads.at[stage], parts.at[slot], part_sem.at[0, slot], part_sem.at[1, slot], device)
+
+    other = 1 - at.side
+    upper = [(at.early, 1, 2 + at.side, at.to_y), (at.early, 2, 2 + other, at.to_corner), (at.late, 0, 2 + other, at.to_x)]
+    lower = [(at.late, 1, at.side, at.to_y), (at.late, 2, other, at.to_corner), (at.early, 0, other, at.to_x)]
+
+    def send_upper():
+        for condition, slot, stage, device in upper:
+            pl.when(condition)(part_copy(slot, stage, device).start)
+
+    def send_lower(which):
+        for condition, slot, stage, device in lower:
+            pl.when(condition & (stage == which))(part_copy(slot, stage, device).start)
+
+    span = GRAD_ROWS // 2
+    mine = pl.ds(pl.multiple_of(at.core * span, 8), span)
+    theirs = pl.ds(pl.multiple_of((1 - at.core) * span, 8), span)
+    near = (at.section, (at.z + 1 - 2 * (at.z % 2)) * 2 + at.core)
+    far = at.to_z(2)
+    trades = [
+        remote(total.at[theirs], halves.at[0], half_sem.at[0, 0], half_sem.at[1, 0], at.to_core),
+        remote(total.at[mine], halves.at[1], half_sem.at[0, 1], half_sem.at[1, 1], near),
+        remote(total.at[mine], halves.at[2], half_sem.at[0, 2], half_sem.at[1, 2], far),
+        remote(final.at[mine], final.at[mine], half_sem.at[0, 3], half_sem.at[1, 3], at.to_core),
+    ]
+
+    def collect():
+        for slot in range(3):
+            part_copy(slot, 0, at.to_x).wait_recv()
+        total[...] = grads[own] + parts[0] + parts[1] + parts[2]
+        trades[0].start()
+
+    def fold(number):
+        def action():
+            trades[number].wait()
+            total[mine] += halves[number]
+            if number < 2:
+                trades[number + 1].start()
+            else:
+                final[mine] = total[mine]
+                trades[3].start()
+
+        return action
+
+    def nothing():
+        pass
+
+    row_in.wait()
+    for copy in keys_in:
+        copy.wait()
+    tasks_through(0)
+    gather.arrive(0)
+    load((0,), 0)
+    for copy in shares:
+        copy.wait()
+    attention_forward(0, 0, [nothing, nothing, take(2)])
+    cot_third.start()
+    tasks_through(2)
+    gather.arrive(1)
+    gather.arrive(2)
+    load((1, 2), 0)
+    ffn_forward(0, [take(1) for _ in range(3)])
+    spills[0].start()
+    pl.when(at.early)(row_own.wait)
+
+    @pl.when(at.late)
+    def _():
+        hid[1] = done[1]
+
+    tasks_through(3)
+    gather.arrive(3)
+    load((0,), middle)
+    attention_forward(1, 1, [take(1) for _ in range(5)])
+    pl.when(at.late)(cot_own.start)
+    load((0,), 1)
+    tasks_through(5)
+    gather.arrive(4)
+    gather.arrive(5)
+    load((1, 2), middle)
+    spills[0].wait()
+    ffn_forward(1, [])
+    spills[1].start()
+    load((1, 2), 1)
+    rows.mail_here(0)
+
+    @pl.when(at.early)
+    def _():
+        hid[2] = done[3]
+
+    attention_forward(2, 2, [])
+    spills[1].wait()
+    ffn_forward(2, [])
+    cot_third.wait()
+    rows.sent(0)
+    ffn_backward(3, 0, nothing)
+    returns[1].start()
+    load((1, 2), middle)
+    attention_backward(3, nothing, [])
+    load((0,), middle)
+    pl.when(at.late)(cot_own.wait)
+
+    @pl.when(at.early)
+    def _():
+        hid[1] = done[0]
+
+    rows.sent(1)
+    returns[1].wait()
+    ffn_backward(4, 1, nothing)
+    returns[0].start()
+    load((1, 2), 0)
+    attention_backward(4, send_upper, [])
+    load((0,), 0)
+    rows.mail_here(3)
+
+    @pl.when(at.late)
+    def _():
+        hid[3] = done[2]
+
+    rows.sent(2)
+    returns[0].wait()
+    ffn_backward(5, 3, lambda: send_lower(1))
+    attention_backward(5, lambda: send_lower(0), [nothing, collect, fold(0), nothing, fold(1), fold(2)])
+    trades[3].wait()
+    result[...] = final[...]
+    for slot in range(3):
+        part_copy(slot, 0, at.to_x).wait_send()
+    for step in range(6):
+        if step >= 3:
+            rows.sent(step)
+        rows.received(step)
+    for unit in range(6):
+        gather.drain(unit)
+
+
+def everything(inputs, cotangent, table, qkv_w, attn_w, in_w, out_w, own_adapter, own_vec, biases, in_bias):
+    length, width = inputs.shape[1:]
+    shard_rows = qkv_w.shape[1]
+    shards = lax.axis_size("dp")
+    count = shards // 2
+    ffn = in_w.shape[2]
+    anyspec = pl.BlockSpec(memory_space=pl.ANY)
+    vmem = pl.BlockSpec(memory_space=pltpu.VMEM)
+    dma = pltpu.SemaphoreType.DMA
+    row = (length, width)
+    scratch = [
+        pltpu.VMEM((4, shards, shard_rows, width), BF16),
+        pltpu.VMEM((4, shards, shard_rows, width), BF16),
+        pltpu.VMEM((4, shards // 4, 4, shard_rows, width), BF16),
+        pltpu.VMEM((3, length, 3 * width), BF16),
+        pltpu.VMEM((3,) + row, BF16),
+        pltpu.VMEM((3, 2) + row, BF16),
+        pltpu.VMEM((3, 2) + row, BF16),
+        pltpu.VMEM((3, 2, length, 128), F32),
+        pltpu.VMEM((length, ffn), BF16),
+        pltpu.VMEM((4,) + row, BF16),
+        pltpu.VMEM((3, length, 128), BF16),
+        pltpu.VMEM((6,) + row, BF16),
+        pltpu.VMEM(row, F32),
+        pltpu.VMEM(row, BF16),
+        pltpu.VMEM((length, 3 * width), BF16),
+        pltpu.VMEM((4, 128, width), BF16),
+        pltpu.VMEM((4, 8, width), F32),
+        pltpu.VMEM((4, GRAD_ROWS, width), F32),
+        pltpu.VMEM((3, GRAD_ROWS, width), F32),
+        pltpu.VMEM((GRAD_ROWS, width), F32),
+        pltpu.VMEM((3, GRAD_ROWS // 2, width), F32),
+        pltpu.VMEM((GRAD_ROWS, width), F32),
+        dma((2, 6, count - 1)),
+        dma((2, 6, count - 1, 2)),
+        dma((2, 6, count - 1, 2)),
+        dma((2, 6, count, 4)),
+        dma((2, 4, 3)),
+        dma((2, 6)),
+        dma((3, 4)),
+        dma((6, 4)),
+        dma((6, 4)),
+        dma((6,)),
+        dma((13,)),
+        dma((2, 3)),
+        dma((2, 4)),
+    ]
+    outs = [
+        (inputs.shape, BF16), (inputs.shape, BF16), ((2, shards, 4, 3, shard_rows, width), BF16),
+        ((2, length, ffn), BF16), ((GRAD_ROWS, width), F32),
+    ]
+    return pl.pallas_call(
+        mega_kernel,
+        in_specs=[anyspec] * 9 + [vmem] * 2,
+        out_specs=[anyspec] * 4 + [vmem],
+        out_shape=[jax.ShapeDtypeStruct(shape, dtype) for shape, dtype in outs],
+        scratch_shapes=scratch,
+        compiler_params=pltpu.CompilerParams(
+            collective_id=1, has_side_effects=True, vmem_limit_bytes=MEGA_BYTES
+        ),
+        cost_estimate=pl.CostEstimate(flops=90_000_000_000, bytes_accessed=200_000_000, transcendentals=0),
+        name="everything",
+    )(inputs, cotangent, table, qkv_w, attn_w, in_w, out_w, own_adapter, own_vec, biases, in_bias)
+
+
 X_PAIRS = [(0, 1), (1, 0), (2, 3), (3, 2)]
 Y_PAIRS = [(0, 2), (2, 0), (1, 3), (3, 1)]
 CROSS = [(0, 3), (3, 0), (1, 2), (2, 1)]
@@ -496,30 +1147,47 @@
             jnp.stack([in_quarters(ffn_in_weight[layer]), outer.reshape((4, -1) + outer.shape[1:])], 1),
         )
 
+    zero_row = jnp.zeros((1, width), F32)
+    own_vec = jnp.concatenate(
+        [zero_row, up_bias, ln_gain, ln_beta, jnp.pad(down_bias, ((0, 0), (0, width - adapter_width))), zero_row, zero_row, zero_row], 0
+    )
+    own_adapter = jnp.concatenate([down_weight[0].T, up_weight[0]], 0)
+    biases = jnp.zeros((layers, 2, 8, width), F32)
+    biases = biases.at[:, 0, 0].set(attn_out_bias).at[:, 0, 5].set(query_bias).at[:, 0, 6].set(value_bias)
+    biases = biases.at[:, 1, 0].set(ffn_out_bias)
+    in_bias = ffn_in_bias[:, None, :]
+    table = key_table(bucket, padding)
+
+    def results(outputs, input_grads, total):
+        ratios = jnp.sqrt(jnp.sum(total[132]) / jnp.sum(total[133]))[None]
+        return (
+            outputs[None],
+            input_grads[None],
+            total[64:128].T[None],
+            total[131, :adapter_width][None],
+            total[0:64][None],
+            total[128][None],
+            total[129][None],
+            total[130][None],
+            ratios,
+        )
+
+    if lax.axis_size("dp") == 8 and lax.axis_size("section") == 4 and inputs.shape[0] == 6:
+        outputs, input_grads, _, _, total = everything(
+            inputs, cotangent, table, qkv_weight, attn_out_weight, ffn_in_weight, ffn_out_weight, own_adapter, own_vec,
+            biases.reshape(2 * layers, 8, width), in_bias,
+        )
+        return results(outputs, input_grads, total)
+
     weights = []
     for layer in range(layers):
-        attn, inner = layer_shards(layer)
-        if layer == 0:
-            attn_full = gather_weights(attn)
-            inner_full = gather_weights(inner)
-            weights.append([block_rows(attn_full, 0, False), block_rows(inner_full, 0, False), block_rows(inner_full, 1, True)])
-        else:
-            full = gather_weights(jnp.concatenate([attn, inner], 1))
-            weights.append([block_rows(full, 0, False), block_rows(full, 1, False), block_rows(full, 2, True)])
-
-    zero_row = jnp.zeros((1, width), F32)
-    own_vecs = jnp.concatenate(
-        [zero_row, up_bias, ln_gain, ln_beta, jnp.pad(down_bias, ((0, 0), (0, width - adapter_width))), zero_row, zero_row, zero_row], 0
-    )
-    own_pack = jnp.concatenate([down_weight[0].T.astype(F32), up_weight[0].astype(F32), own_vecs], 0)
-    packs = lax.all_gather(own_pack, "section", axis=0, tiled=False)
-    adapters = packs[:, :128].astype(BF16).reshape(layers, 2, 128, width)
-    vecs = packs[:, 128:].reshape(layers, 2, 8, width)
-    vecs = vecs.at[:, 0, 0].set(attn_out_bias).at[:, 0, 5].set(query_bias).at[:, 0, 6].set(value_bias)
-    vecs = vecs.at[:, 1, 0].set(ffn_out_bias).reshape(layers, 16, width)
-    in_bias = ffn_in_bias[:, None, :]
-
-    table = key_table(bucket, padding)
+        full = gather_weights(jnp.concatenate(layer_shards(layer), 1))
+        weights.append([block_rows(full, 0, False), block_rows(full, 1, False), block_rows(full, 2, True)])
+    adapters = lax.all_gather(own_adapter, "section", axis=0, tiled=False)
+    vecs = lax.all_gather(own_vec, "section", axis=0, tiled=False)
+    adapters = adapters.reshape(layers, 2, 128, width)
+    vecs = vecs.reshape(layers, 2, 8, width)
+    vecs = (vecs + biases).reshape(layers, 16, width)
     own = section
     shared = 4 + side
 
@@ -600,26 +1268,13 @@
     )
 
     def with_sums(grads, sums):
-        squares = jnp.sum(sums[:4].reshape(2, 2, width), -1, keepdims=True)
-        return grads.at[:, 132:134].set(jnp.broadcast_to(squares, (2, 2, width)))
+        return grads.at[:, 132:134].set(sums[:4].reshape(2, 2, width))
 
     g3, g4, g5 = with_sums(b3[2], f2[11]), with_sums(b4[2], f1[11]), with_sums(b5[2], f0[11])
     low_layer = g5 + jnp.where(early, g4, 0.0)
     high_layer = g3 + jnp.where(early, 0.0, g4)
     mine = lax.psum_scatter(jnp.concatenate([low_layer, high_layer], 0), "section", scatter_dimension=0, tiled=False)
-    total = lax.psum(mine, "dp")
-    ratios = jnp.sqrt(total[132, 0] / total[133, 0])[None]
-    return (
-        outputs[None],
-        input_grads[None],
-        total[64:128].T[None],
-        total[131, :adapter_width][None],
-        total[0:64][None],
-        total[128][None],
-        total[129][None],
-        total[130][None],
-        ratios,
-    )
+    return results(outputs, input_grads, lax.psum(mine, "dp"))
 
 
 def solution(mesh):

time: 681 us -> 485 us (0.71)
  waiting for transfers between devices: 336 us -> 0 us
  Pallas kernels: 207 us -> 445 us
  starting transfers between devices: 31.1 us -> 0 us
  other arithmetic: 44.7 us -> 15.1 us
  local copies, waits for them, and re-layouts: 41.8 us -> 16.8 us
  between operations: 17.5 us -> 3.46 us
    pallas_call x6 -> x1, Pallas kernels: 207 us -> 445 us  [everything(): pl.pallas_call(mega_kernel, in_specs=[anyspec] * 9 + [vmem] * 2, out_spec...]
    all_gather x4 -> x0, waiting for transfers between devices: 224 us -> none  [the longest x3 215 us: gather_weights(): full = lax.all_gather(quarter, ('dp', 'section'), axis=0, tiled=False)]
    ppermute x14 -> x0, waiting for transfers between devices: 57.2 us -> none  [send(): lax.ppermute(value, 'section', [pair for pair in pairs if pair[0] in send...]
    psum x1 -> x0, waiting for transfers between devices: 54.2 us -> none  [on_device(): total = lax.psum(mine, 'dp')]
    ppermute x14 -> x0, starting transfers between devices: 30.8 us -> none  [send(): lax.ppermute(value, 'section', [pair for pair in pairs if pair[0] in send...]
    select_n x6 -> x0, other arithmetic: 13.7 us -> none  [the longest x1 3.32 us: on_device(): z3 = send(jnp.where(side == 0, b3[0], b3[1]), CROSS, (0, 1))]
    dynamic_update_slice x10 -> x0, other arithmetic: 13.5 us -> none  [assemble(): result = lax.dynamic_update_index_in_dim(result, part, row, 0)]
    another operation x8 -> x2, other arithmetic: 9.13 us -> 1.38 us
  transfers between devices with their start and end apart: 20 -> 0, of which waited for: 7 -> 0; matrix products, arithmetic and copies ran while one was open for 11% -> 0% of each run, Pallas kernels for 31% -> 0%
where the time goes in v3:
time: 485 us; the launch traced here: 481 us
  Pallas kernels  445 us (92%)
  local copies, waits for them, and re-layouts  16.8 us (3%)
  other arithmetic  15.1 us (3%)
    pallas_call x1, Pallas kernels, everything(): pl.pallas_call(mega_kernel, in_specs=[anyspec] * 9 + [vmem] * 2, out_spec...  445 us

profile of v3, /device:TPU:0, one launch (start us, length us, event | category | flops | bytes accessed | tf_op | source)
XLA Modules:
  0.0 480.5 jit_solution(5009713203892848374)
XLA Ops:
  0.6 0.7 broadcast_add_fusion
  1.3 0.6 fusion.4
  1.9 1.4 and_reduce_fusion
  3.3 0.6 fusion.5
  3.9 0.7 pad.21
  4.5 0.1 broadcast_shift-right-arithmetic_fusion
  4.6 1.4 concatenate.26.own_vec
  6.0 0.7 fusion.3
  6.7 0.1 iota_shift-right-arithmetic_fusion
  6.8 1.4 broadcast_in_dim.71.in_bias
  8.1 0.7 scatter.14
  8.8 2.7 fusion.1
  11.5 2.6 fusion.2
  14.1 0.7 bitcast_dynamic-update-slice_fusion
  14.8 0.6 copy.28
  15.5 1.6 pad_maximum_fusion.own_adapter
  17.1 3.1 select_convert_fusion.table
  20.2 445.1 %everything.1 = (bf16[6,512,768]{2,1,0:T(8,128)(2,1)}, bf16[6,512,768]{2,1,0:T(8,128)(2,1)}, bf16[2,8,4,3,96,768]{5,4,3,2,1,0:T(8,128)(2,1)}, bf16[2,512,3072]{2,1,0:T(8,128)(2,1)}, f32[144,768]{1,0:T(8,128)}) custom-call(bf16[6,512,768]{2,1,0:T(8,128)(2,1)} %inputs.1, bf16[6,512,768]{2,1,0:T(8,128)(2,1)} %cotangent.1, ...), custom_call_target="tpu_custom_call" | custom-call | flops 89999998976 | bytes 200000000 | tf_op jit(solution)/shard_map/everything/pallas_call | solution.py:1084
  465.3 1.2 slice.148
  466.5 2.2 slice_reduce_fusion
  470.1 0.0 slice-start
  470.1 1.9 slice_bitcast_fusion
  472.0 0.0 slice-start.1
  472.0 4.9 %copy.34 = bf16[1,6,512,768]{3,2,1,0:T(8,128)(2,1)} copy(bf16[1,6,512,768]{3,2,1,0:T(8,128)(2,1)} %bitcast.30) | data formatting | bytes 9437184
  476.9 0.0 slice-done
  476.9 0.0 slice-done.1
  476.9 2.2 copy.35
  (7 shorter events, 0.0 us)
Async XLA Ops:
  470.1 6.8 %slice-start = ((s8[4718592]{0:T(1024)(128)(4,1)}), s8[4194304]{0:T(1024)(128)(4,1)S(1)}, s32[]{:S(2)}) async-start(s8[4718592]{0:T(1024)(128)(4,1)} %bitcast.27), calls=%async_computation | async-start | bytes 8388608
  472.0 4.9 %slice-start.1 = ((s8[4718592]{0:T(1024)(128)(4,1)}), s8[524288]{0:T(1024)(128)(4,1)S(1)}, s32[]{:S(2)}) async-start(s8[4718592]{0:T(1024)(128)(4,1)} %bitcast.27), calls=%async_computation.1 | async-start | bytes 1048576
